TPU v7x, 32 devices: a whole 2x2x4 slice. The times are simulated.
32 devices in a mesh: lat: 8 (over z, y), tp: 4 (over x, core).
Axes of the slice: x: 2, y: 2, z: 4, core: 2. Of those that a mesh axis runs over, the one named last changes fastest.
Arguments:
- activations: bfloat16 [2048, 7168], P('lat', 'tp'), may hold values from -16 to 16, as said below
- active_blocks: int32 [2048, 2], P('lat'), may hold values from 0 to 7, all different within a row; in each aligned block of 256 rows (0 to 255, 256 to 511, ...) at most 128 rows name the same one
- enc_weight: bfloat16 [7168, 16384], P('tp', 'lat'), may hold values from -0.0625 to 0.0625
- enc_bias: float32 [16384], P('lat'), may hold values from -3 to 3
- dec_weight: bfloat16 [16384, 7168], P('lat', 'tp'), may hold values from -0.125 to 0.125
- dec_bias: float32 [7168], P('tp'), may hold values from -3 to 3
Outputs:
- token_error: float32 [2048], P('lat')
- mean_error: float32 [], replicated
Inputs may be any that keep to these rules, and one draw needn't show every extreme that they name: `active_blocks`: each row names 2 different blocks; among the rows of one index of lat no block is named more than 128 times, and some block is named exactly 128 times. `activations`: real values.
All inputs are finite; a program needn't handle non-finite values.
Results may differ from a plain program's by a relative error of at most 0.005.
Values may be sent and summed in bfloat16 or wider, within the bound.
A program may use at most 64 MiB of HBM per device.

v0:
```python
import jax
import jax.numpy as jnp
from jax import lax
from jax.sharding import PartitionSpec as P


def score_slots(received, enc_weight, enc_bias, dec_weight):
    owners = received.shape[0]
    slot_count = received.shape[1]
    feature_part = received.shape[2]
    flat_rows = received.reshape(owners * slot_count, feature_part)
    partial_value = jnp.dot(flat_rows, enc_weight, preferred_element_type=jnp.float32)
    pre = lax.psum(partial_value.astype(jnp.bfloat16), "tp").astype(jnp.float32)
    latents = jnp.maximum(pre + enc_bias, 0.0).astype(jnp.bfloat16)
    decoded = jnp.dot(latents, dec_weight, preferred_element_type=jnp.float32).astype(jnp.bfloat16)
    decoded = decoded.reshape(owners, slot_count, feature_part)
    return lax.all_to_all(decoded, "lat", split_axis=0, concat_axis=0, tiled=True)


def body(activations, active_blocks, enc_weight, enc_bias, dec_weight, dec_bias):
    owners = lax.axis_size("lat")
    token_count, active_count = active_blocks.shape
    feature_part = activations.shape[1]
    capacity = 2 * token_count * active_count // owners
    centred = (activations.astype(jnp.float32) - dec_bias).astype(jnp.bfloat16)
    flat = active_blocks.reshape(-1)
    onehot = (flat[:, None] == jnp.arange(owners, dtype=jnp.int32)[None, :]).astype(jnp.int32)
    ranks = jnp.sum((jnp.cumsum(onehot, axis=0) - onehot) * onehot, axis=1)
    slot_rows = flat * capacity + ranks
    source_rows = jnp.repeat(centred, active_count, axis=0)
    outgoing = (
        jnp.zeros((owners * capacity, feature_part), jnp.bfloat16).at[slot_rows].set(source_rows)
    )
    outgoing = outgoing.reshape(owners, capacity, feature_part)
    received = lax.all_to_all(outgoing, "lat", split_axis=0, concat_axis=0, tiled=True)
    returned = score_slots(received, enc_weight, enc_bias, dec_weight)
    returned = returned.reshape(owners * capacity, feature_part)
    picked = returned[slot_rows].reshape(token_count, active_count, feature_part)
    recon = jnp.sum(picked.astype(jnp.float32), axis=1) + dec_bias
    inputs_full = activations.astype(jnp.float32)
    diff = inputs_full - recon
    squares, norms = lax.psum(
        (jnp.sum(diff * diff, axis=1), jnp.sum(inputs_full * inputs_full, axis=1)), "tp"
    )
    token_error = squares / (norms + 1e-06)
    total = lax.psum(jnp.sum(token_error), "lat")
    mean_error = total / (token_count * owners)
    return (token_error, mean_error)


def solution(mesh):
    in_specs = (P("lat", "tp"), P("lat", None), P("tp", "lat"), P("lat"), P("lat", "tp"), P("tp"))
    out_specs = (P("lat"), P())
    return jax.shard_map(body, mesh=mesh, in_specs=in_specs, out_specs=out_specs, check_vma=False)
```

profile of v0, /device:TPU:0, one launch (start us, length us, event | category | flops | bytes accessed | tf_op | source)
XLA Modules:
  0.0 359.7 jit_solution(12493566619651731548)
XLA Ops:
  7.2 0.0 all-reduce.3.cloned.1.call-start
  7.2 0.8 copy.9
  8.0 0.1 eq.29
  8.2 0.1 eq.25
  8.3 0.7 broadcast_multiply_fusion
  9.0 1.1 reduce-window.6
  10.1 0.2 slice_reduce_fusion
  10.4 0.1 copy.8
  10.5 0.1 mul.27
  10.7 1.3 fusion.4
  12.0 0.9 broadcast_in_dim.5
  13.0 1.7 reshape.89
  14.6 0.1 fusion.11
  14.7 6.6 %scatter_custom_fusion = bf16[1024,1792]{1,0:T(8,128)(2,1)} fusion(s32[512]{0:T(512)S(1)} %bitcast.20, bf16[512,1792]{1,0:T(8,128)(2,1)} %reshape.89, bf16[]{:T(256)} %constant.7.clone.1), kind=kCustom, calls=%fused_computation.15 | custom fusion | bytes 3670528 | tf_op jit(solution)/shard_map/scatter | solution.py:32
  21.3 89.2 %all_to_all.10 = bf16[8,128,1792]{2,1,0:T(8,128)(2,1)S(1)} all-to-all(bf16[8,128,1792]{2,1,0:T(8,128)(2,1)} %bitcast.17), channel_id=1, replica_groups=mesh['lat'=8,'tp'=4] {'lat'}, dimensions={0} | all-to-all | bytes 7340032 | tf_op jit(solution)/shard_map/all_to_all | solution.py:35
  110.5 11.4 %convolution_convert_fusion = bf16[1024,2048]{1,0:T(8,128)(2,1)} fusion(bf16[1024,1792]{1,0:T(8,128)(2,1)S(1)} %bitcast.19, bf16[1792,2048]{1,0:T(8,128)(2,1)} %param.8), kind=kOutput, calls=%fused_computation.7 | convolution fusion | flops 7518289920 | bytes 15204352 | tf_op jit(solution)/shard_map/dot_general | solution.py:12
  121.9 0.0 copy-start.2
  121.9 0.0 all-reduce.3.cloned.1.call-update
  121.9 84.7 %all-reduce.3.cloned.1.call-done = bf16[1024,2048]{1,0:T(8,128)(2,1)} async-done(((bf16[1024,2048]{1,0:T(8,128)(2,1)}), bf16[1024,2048]{1,0:T(8,128)(2,1)}) %all-reduce.3.cloned.1.call-update) | async-done | bytes 4194320 | tf_op jit(solution)/shard_map/psum | solution.py:13
  206.6 0.0 copy-done.2
  206.6 12.9 %fusion.3 = bf16[1024,1792]{1,0:T(8,128)(2,1)} fusion(bf16[2048,1792]{1,0:T(8,128)(2,1)} %param.10, bf16[1024,2048]{1,0:T(8,128)(2,1)} %all-reduce.3.cloned.1.call-done, f32[2048]{0:T(1024)S(1)} %copy-done.2), kind=kOutput, calls=%fused_computation.6 | convolution fusion | flops 7526416384 | bytes 15212544 | tf_op jit(solution)/shard_map/dot_general | solution.py:15
  219.5 5.5 %all-to-all-start.1 = ((bf16[8,128,1792]{2,1,0:T(8,128)(2,1)}), bf16[8,128,1792]{2,1,0:T(8,128)(2,1)}, u32[]{:S(2)}, u32[]{:S(2)}) async-start(bf16[8,128,1792]{2,1,0:T(8,128)(2,1)} %bitcast.18), calls=%async_computation.1 | async-start | bytes 7340032 | tf_op jit(solution)/shard_map/all_to_all | solution.py:17
  225.0 81.9 %all-to-all-done.1 = bf16[8,128,1792]{2,1,0:T(8,128)(2,1)} async-done(((bf16[8,128,1792]{2,1,0:T(8,128)(2,1)}), bf16[8,128,1792]{2,1,0:T(8,128)(2,1)}, u32[]{:S(2)}, u32[]{:S(2)}) %all-to-all-start.1) | async-done | bytes 3670048 | tf_op jit(solution)/shard_map/all_to_all | solution.py:17
  306.9 6.5 %gather_fusion = bf16[512,1792]{1,0:T(8,128)(2,1)S(1)} fusion(bf16[1024,1792]{1,0:T(8,128)(2,1)} %bitcast.7, s32[1024]{0:T(1024)S(1)} %pad_clamp_fusion), kind=kCustom, calls=%fused_computation | custom fusion | bytes 3672064 | tf_op jit(solution)/shard_map/gather | solution.py:38
  313.4 3.0 reshape.76
  316.4 6.5 %reduce_sum.49 = f32[256,1792]{1,0:T(8,128)S(1)} reduce(f32[256,2,1792]{2,1,0:T(2,128)} %reshape.76, f32[]{:T(128)} %constant.5.clone.1), dimensions={1}, to_apply=%region_5.6 | reduce | flops 458752 | bytes 5505028 | tf_op jit(solution)/shard_map/reduce_sum | solution.py:39
  322.9 0.0 copy-done
  322.9 0.0 copy-done.1
  322.9 0.5 fusion.7
  323.4 5.7 %all-reduce = (f32[256]{0:T(256)S(1)}, f32[256]{0:T(256)S(1)}) all-reduce(f32[256]{0:T(256)S(1)} %get-tuple-element.3, f32[256]{0:T(256)S(1)} %get-tuple-element.2), channel_id=1, replica_groups=mesh['lat'=8,'tp'=4] {'tp'}, use_global_device_ids=true, to_apply=%region_7.8 | all-reduce | flops 512 | bytes 4096 | tf_op jit(solution)/shard_map/psum | solution.py:42
  329.0 1.2 fusion.14
  330.2 20.8 %psum.31 = f32[]{:T(128)} all-reduce(f32[]{:T(128)} %get-tuple-element.6), channel_id=1, replica_groups=mesh['lat'=8,'tp'=4] {'lat'}, use_global_device_ids=true, to_apply=%region_11.12 | all-reduce | flops 1 | bytes 8 | tf_op jit(solution)/shard_map/psum | solution.py:46
  (7 shorter events, 0.1 us)
Async XLA Ops:
  7.2 199.4 %all-reduce.3.cloned.1.call-start = ((), (), s32[]{:S(2)}) async-start(), calls=%async_computation.2 | async-start | bytes 8388608 | tf_op jit(solution)/shard_map/psum | solution.py:13
  121.9 84.7 %copy-start.2 = (f32[2048]{0:T(1024)S(1)}, f32[2048]{0:T(1024)}, u32[]{:S(2)}) copy-start(f32[2048]{0:T(1024)} %param.9) | copy-start | bytes 24580
  219.5 87.4 %all-to-all-start.1 = ((bf16[8,128,1792]{2,1,0:T(8,128)(2,1)}), bf16[8,128,1792]{2,1,0:T(8,128)(2,1)}, u32[]{:S(2)}, u32[]{:S(2)}) async-start(bf16[8,128,1792]{2,1,0:T(8,128)(2,1)} %bitcast.18), calls=%async_computation.1 | async-start | bytes 7340032 | tf_op jit(solution)/shard_map/all_to_all | solution.py:17
  316.4 6.5 %copy-start = (bf16[256,1792]{1,0:T(8,128)(2,1)S(1)}, bf16[256,1792]{1,0:T(8,128)(2,1)}, u32[]{:S(2)}) copy-start(bf16[256,1792]{1,0:T(8,128)(2,1)} %param.6) | copy-start | bytes 2752516
  316.4 6.5 %copy-start.1 = (f32[1792]{0:T(1024)S(1)}, f32[1792]{0:T(1024)}, u32[]{:S(2)}) copy-start(f32[1792]{0:T(1024)} %param.11) | copy-start | bytes 21508
Sparse Core Ops, SparseCore 0:
  122.0 84.4 all-reduce.2
where the time goes:
time: 360 us
  waiting for transfers between devices  167 us (46%)
  blocking collectives  116 us (32%)
  matrix products  24.3 us (7%)
  local copies, waits for them, and re-layouts  20.3 us (6%)
  between operations  15.9 us (4%)
  other arithmetic  11.4 us (3%)
  starting transfers between devices  5.55 us (2%)
    all_to_all x1, blocking collectives, body(): lax.all_to_all(outgoing, 'lat', split_axis=0, concat_axis=0, tiled=True)  89.2 us
    psum x1, waiting for transfers between devices, score_slots(): pre = lax.psum(partial_value.astype(jnp.bfloat16), 'tp').astype(jnp.float32)  84.7 us
    all_to_all x1, waiting for transfers between devices, score_slots(): lax.all_to_all(decoded, 'lat', split_axis=0, concat_axis=0, tiled=True)  81.9 us
    psum x1, blocking collectives, body(): total = lax.psum(jnp.sum(token_error), 'lat')  20.8 us
    dot_general x1, matrix products, score_slots(): jnp.dot(latents, dec_weight, preferred_element_type=jnp.float32)  12.9 us
    dot_general x1, matrix products, score_slots(): jnp.dot(flat_rows, enc_weight, preferred_element_type=jnp.float32)  11.4 us
  transfers between devices with their start and end apart: 2, of which 2 were waited for; matrix products, arithmetic and copies ran while one was open for 0% of the time, Pallas kernels for 0%

commit v1 on v0

--- a/solution.py
+++ b/solution.py
@@ -17,7 +17,21 @@
     return lax.all_to_all(decoded, "lat", split_axis=0, concat_axis=0, tiled=True)
 
 
-def body(activations, active_blocks, enc_weight, enc_bias, dec_weight, dec_bias):
+def finish(activations, summed, dec_bias, owners):
+    token_count = activations.shape[0]
+    recon = summed + dec_bias
+    inputs_full = activations.astype(jnp.float32)
+    diff = inputs_full - recon
+    squares, norms = lax.psum(
+        (jnp.sum(diff * diff, axis=1), jnp.sum(inputs_full * inputs_full, axis=1)), "tp"
+    )
+    token_error = squares / (norms + 1e-06)
+    total = lax.psum(jnp.sum(token_error), "lat")
+    mean_error = total / (token_count * owners)
+    return (token_error, mean_error)
+
+
+def general_body(activations, active_blocks, enc_weight, enc_bias, dec_weight, dec_bias):
     owners = lax.axis_size("lat")
     token_count, active_count = active_blocks.shape
     feature_part = activations.shape[1]
@@ -36,19 +50,150 @@
     returned = score_slots(received, enc_weight, enc_bias, dec_weight)
     returned = returned.reshape(owners * capacity, feature_part)
     picked = returned[slot_rows].reshape(token_count, active_count, feature_part)
-    recon = jnp.sum(picked.astype(jnp.float32), axis=1) + dec_bias
-    inputs_full = activations.astype(jnp.float32)
-    diff = inputs_full - recon
-    squares, norms = lax.psum(
-        (jnp.sum(diff * diff, axis=1), jnp.sum(inputs_full * inputs_full, axis=1)), "tp"
-    )
-    token_error = squares / (norms + 1e-06)
-    total = lax.psum(jnp.sum(token_error), "lat")
-    mean_error = total / (token_count * owners)
-    return (token_error, mean_error)
+    return finish(activations, jnp.sum(picked.astype(jnp.float32), axis=1), dec_bias, owners)
+
+
+def pairs(*hops):
+    return [(2 * a + c, 2 * b + c) for a, b in hops for c in range(2)]
+
+
+TO_INNER = pairs((0, 1), (3, 2))
+TO_OUTER = pairs((1, 0), (2, 3))
+ACROSS = pairs((1, 2), (2, 1))
+COLUMN = [(i, i ^ 1) for i in range(8)]
+CORE = [(i, i ^ 1) for i in range(4)]
+SIDE = [(i, i ^ 2) for i in range(4)]
+OUT_PARTS = 2
+
+
+def to_inner(x):
+    return lax.ppermute(x, "lat", TO_INNER)
+
+
+def to_outer(x):
+    return lax.ppermute(x, "lat", TO_OUTER)
+
+
+def across(x):
+    return lax.ppermute(x, "lat", ACROSS)
+
+
+def swap_column(x):
+    return lax.ppermute(x, "lat", COLUMN)
+
+
+def line_body(activations, active_blocks, enc_weight, enc_bias, dec_weight, dec_bias):
+    owners = 8
+    tokens, active_count = active_blocks.shape
+    capacity = 2 * tokens * active_count // owners
+    width = activations.shape[1]
+    block = enc_weight.shape[1]
+    half = block // 2
+    me = lax.axis_index("lat")
+    plane, column = me // 2, me % 2
+    inner = (plane == 1) | (plane == 2)
+    low = plane < 2
+    core = lax.axis_index("tp") % 2
+
+    centred = (activations.astype(jnp.float32) - dec_bias).astype(jnp.bfloat16)
+    named_by = lax.all_gather(active_blocks, "lat")
+
+    from_outer = to_inner(centred)
+    from_inner = to_outer(centred)
+    from_across = across(centred)
+    from_inner2 = to_outer(from_across)
+    from_across2 = across(from_outer)
+    from_inner3 = to_outer(from_across2)
+    sources = [
+        jnp.where(inner, centred, from_inner),
+        jnp.where(inner, from_across, from_inner2),
+        jnp.where(inner, from_outer, centred),
+        jnp.where(inner, from_across2, from_inner3),
+    ]
+    near_inner = jnp.where(low, 1, 2)
+    near_outer = jnp.where(low, 0, 3)
+    order = jnp.stack([near_inner, 3 - near_inner, near_outer, 3 - near_outer])
+    blocks_of = named_by[order * 2 + column]
+    wanted = jnp.stack([me, me ^ 1])
+    named = jnp.any(blocks_of[:, None] == wanted[None, :, None, None], axis=-1)
+    earlier = jnp.arange(tokens)[:, None] < jnp.arange(tokens)[None, :]
+    ranks = jnp.dot(
+        named.reshape(8, tokens).astype(jnp.bfloat16),
+        earlier.astype(jnp.bfloat16),
+        preferred_element_type=jnp.float32,
+    ).astype(jnp.int32).reshape(4, 2, 1, tokens)
+    slots = jnp.arange(capacity, dtype=jnp.int32)[None, None, :, None]
+    picks = ((ranks == slots) & named[:, :, None, :]).astype(jnp.bfloat16)
+    picks = picks.reshape(4, 2 * capacity, tokens)
+
+    bias_half = lax.dynamic_slice_in_dim(enc_bias, core * half, half)
+
+    def pick(first):
+        rows = [
+            jnp.dot(picks[i], sources[i], preferred_element_type=jnp.float32).astype(jnp.bfloat16)
+            for i in (first, first + 1)
+        ]
+        mine = jnp.concatenate([r[:capacity] for r in rows])
+        theirs = jnp.concatenate([r[capacity:] for r in rows])
+        return mine, swap_column(theirs)
+
+    def encode(mine, received):
+        rows = jnp.concatenate([mine, received])
+        part = jnp.dot(rows, enc_weight, preferred_element_type=jnp.float32).astype(jnp.bfloat16)
+        left, right = part[:, :half], part[:, half:]
+        kept = jnp.where(core == 0, left, right)
+        given = jnp.where(core == 0, right, left)
+        other = lax.ppermute(given, "tp", CORE)
+        chip = (kept.astype(jnp.float32) + other.astype(jnp.float32)).astype(jnp.bfloat16)
+        side = lax.ppermute(chip, "tp", SIDE)
+        pre = chip.astype(jnp.float32) + side.astype(jnp.float32) + bias_half
+        own = jnp.maximum(pre, 0.0).astype(jnp.bfloat16)
+        sibling = lax.ppermute(own, "tp", CORE)
+        return jnp.concatenate(
+            [jnp.where(core == 0, own, sibling), jnp.where(core == 0, sibling, own)], axis=1
+        )
+
+    def decode(latents, first, weight):
+        decoded = jnp.dot(latents, weight, preferred_element_type=jnp.float32).astype(jnp.bfloat16)
+        back = swap_column(decoded[2 * capacity:])
+        sums = []
+        for i in range(2):
+            own = decoded[i * capacity:(i + 1) * capacity]
+            other = back[i * capacity:(i + 1) * capacity]
+            placed = lax.dot_general(
+                picks[first + i],
+                jnp.concatenate([own, other]),
+                (((0,), (0,)), ((), ())),
+                preferred_element_type=jnp.float32,
+            )
+            sums.append(placed.astype(jnp.bfloat16))
+        return sums
+
+    def add(a, b):
+        return (a.astype(jnp.float32) + b.astype(jnp.float32)).astype(jnp.bfloat16)
+
+    latents_inner = encode(*pick(0))
+    latents_outer = encode(*pick(2))
+    summed = []
+    step = width // OUT_PARTS
+    for p in range(OUT_PARTS):
+        weight = dec_weight[:, p * step:(p + 1) * step]
+        near, far = decode(latents_inner, 0, weight)
+        far1 = to_inner(far)
+        far2 = across(add(far, far1))
+        near1 = to_inner(near)
+        at_inner = near.astype(jnp.float32) + far2.astype(jnp.float32) + near1.astype(jnp.float32)
+        own, end = decode(latents_outer, 2, weight)
+        end1 = to_inner(end)
+        end2 = across(add(end, end1))
+        end3 = to_outer(add(own, end2))
+        at_outer = own.astype(jnp.float32) + end3.astype(jnp.float32)
+        summed.append(jnp.where(inner, at_inner, at_outer))
+    return finish(activations, jnp.concatenate(summed, axis=1), dec_bias, owners)
 
 
 def solution(mesh):
     in_specs = (P("lat", "tp"), P("lat", None), P("tp", "lat"), P("lat"), P("lat", "tp"), P("tp"))
     out_specs = (P("lat"), P())
+    body = line_body if (mesh.shape["lat"], mesh.shape["tp"]) == (8, 4) else general_body
     return jax.shard_map(body, mesh=mesh, in_specs=in_specs, out_specs=out_specs, check_vma=False)

time: 360 us -> 324 us (0.900)
  blocking collectives: 116 us -> 70.5 us
  starting transfers between devices: 5.55 us -> 35.8 us
  local copies, waits for them, and re-layouts: 20.3 us -> 1.54 us
  between operations: 15.9 us -> 3.22 us
  waiting for transfers between devices: 167 us -> 177 us
    ppermute x0 -> x30, waiting for transfers between devices: none -> 177 us  [the longest x5 60.6 us: to_outer(): return lax.ppermute(x, 'lat', TO_OUTER)]
    all_to_all x1 -> x0, blocking collectives: 89.2 us -> none  [body(): lax.all_to_all(outgoing, 'lat', split_axis=0, concat_axis=0, tiled=True)]
    psum x1 -> x0, waiting for transfers between devices: 84.7 us -> none  [score_slots(): pre = lax.psum(partial_value.astype(jnp.bfloat16), 'tp').astype(jnp.float32)]
    all_to_all x1 -> x0, waiting for transfers between devices: 81.9 us -> none  [score_slots(): lax.all_to_all(decoded, 'lat', split_axis=0, concat_axis=0, tiled=True)]
    all_gather x0 -> x1, blocking collectives: none -> 43.1 us  [line_body(): named_by = lax.all_gather(active_blocks, 'lat')]
    ppermute x0 -> x30, starting transfers between devices: none -> 35.8 us  [the longest x7 16.8 us: to_inner(): return lax.ppermute(x, 'lat', TO_INNER)]
    scatter x1 -> x0, local copies, waits for them, and re-layouts: 6.58 us -> none  [body(): jnp.zeros((owners * capacity, feature_part), jnp.bfloat16).at[slot_rows]]
    reduce_sum x4 -> x2, other arithmetic: 8.22 us -> 1.72 us  [the longest x1 1.17 us: finish(): total = lax.psum(jnp.sum(token_error), 'lat')]
  transfers between devices with their start and end apart: 2 -> 30, of which waited for: 2 -> 16; matrix products, arithmetic and copies ran while one was open for 0% -> 8% of each run, Pallas kernels for 0% -> 0%
where the time goes in v1:
time: 324 us; the launch traced here: 323 us
  waiting for transfers between devices  177 us (55%)
  blocking collectives  70.5 us (22%)
  starting transfers between devices  35.8 us (11%)
  matrix products  25.9 us (8%)
  other arithmetic  8.91 us (3%)
    ppermute x5, waiting for transfers between devices, to_outer(): return lax.ppermute(x, 'lat', TO_OUTER)  60.6 us
    ppermute x6, waiting for transfers between devices, swap_column(): return lax.ppermute(x, 'lat', COLUMN)  45 us
    ppermute x2, waiting for transfers between devices, encode(): side = lax.ppermute(chip, 'tp', SIDE)  44 us
    all_gather x1, blocking collectives, line_body(): named_by = lax.all_gather(active_blocks, 'lat')  43.1 us
    ppermute x7, waiting for transfers between devices, to_inner(): return lax.ppermute(x, 'lat', TO_INNER)  25.1 us
    psum x1, blocking collectives, finish(): total = lax.psum(jnp.sum(token_error), 'lat')  21.8 us
    ppermute x7, starting transfers between devices, to_inner(): return lax.ppermute(x, 'lat', TO_INNER)  16.8 us
    dot_general x4, matrix products, decode(): jnp.dot(latents, weight, preferred_element_type=jnp.float32)  11.5 us
  transfers between devices with their start and end apart: 30, of which 16 were waited for; matrix products, arithmetic and copies ran while one was open for 8% of the time, Pallas kernels for 0%

profile of v1, /device:TPU:0, one launch (start us, length us, event | category | flops | bytes accessed | tf_op | source)
XLA Modules:
  0.0 323.2 jit_solution(18417472798483882288)
XLA Ops:
  2.0 5.0 %collective-permute-start.11 = (bf16[256,1792]{1,0:T(8,128)(2,1)S(1)}, bf16[256,1792]{1,0:T(8,128)(2,1)S(1)}, u32[]{:S(2)}, u32[]{:S(2)}) collective-permute-start(bf16[256,1792]{1,0:T(8,128)(2,1)S(1)} %fusion.8), channel_id=1, source_target_pairs={{0,8},{4,12},{24,16},{28,20},{1,9},{5,13},{25,17},{29,21},{2,10},{... | collective-permute-start | bytes 2752520 | tf_op jit(solution)/shard_map/ppermute | solution.py:70
  9.1 43.1 %all-gather = s32[2048,2]{0,1:T(2,128)S(1)} all-gather(s32[256,2]{0,1:T(2,128)} %param.7), channel_id=2, replica_groups=mesh['lat'=8,'tp'=4] {'lat'}, dimensions={0}, use_global_device_ids=true | all-gather | bytes 18432 | tf_op jit(solution)/shard_map/all_gather | solution.py:99
  56.0 1.6 convolution_convert_fusion.5
  59.4 19.4 %collective-permute-done.2 = bf16[256,1792]{1,0:T(8,128)(2,1)S(1)} collective-permute-done((bf16[256,1792]{1,0:T(8,128)(2,1)S(1)}, bf16[256,1792]{1,0:T(8,128)(2,1)S(1)}, u32[]{:S(2)}, u32[]{:S(2)}) %collective-permute-start.2) | collective-permute-done | bytes 917536 | tf_op jit(solution)/shard_map/ppermute | solution.py:74
  79.5 12.9 %collective-permute-done.13 = bf16[256,1792]{1,0:T(8,128)(2,1)S(1)} collective-permute-done((bf16[256,1792]{1,0:T(8,128)(2,1)S(1)}, bf16[256,1792]{1,0:T(8,128)(2,1)S(1)}, u32[]{:S(2)}, u32[]{:S(2)}) %collective-permute-start.13) | collective-permute-done | bytes 917536 | tf_op jit(solution)/shard_map/ppermute | solution.py:74
  93.0 3.1 collective-permute-done.3
  96.1 4.1 %convolution_convert_fusion.1 = bf16[512,2048]{1,0:T(8,128)(2,1)S(1)} fusion(bf16[1792,2048]{1,0:T(8,128)(2,1)S(1)} %bitcast.42, bf16[256,1792]{1,0:T(8,128)(2,1)S(1)} %collective-permute-done.3, bf16[128,1792]{1,0:T(8,128)(2,1)S(1)} %get-tuple-element.20, bf16[128,1792]{1,0:T(8,128)(2,1)S(1)} %get-tuple-element.18), kind=kOutput, calls=%fused_computation.10 | convolution fusion | flops 3764649984 | bytes 11272192 | tf_op jit(solution)/shard_map/dot_general | solution.py:142
  100.4 12.1 %collective-permute-done.14 = bf16[256,1792]{1,0:T(8,128)(2,1)S(1)} collective-permute-done((bf16[256,1792]{1,0:T(8,128)(2,1)S(1)}, bf16[256,1792]{1,0:T(8,128)(2,1)S(1)}, u32[]{:S(2)}, u32[]{:S(2)}) %collective-permute-start.14) | collective-permute-done | bytes 917536 | tf_op jit(solution)/shard_map/ppermute | solution.py:82
  112.5 4.3 %convolution_convert_fusion = bf16[512,2048]{1,0:T(8,128)(2,1)S(1)} fusion(bf16[1792,2048]{1,0:T(8,128)(2,1)S(1)} %bitcast.42, bf16[256,1792]{1,0:T(8,128)(2,1)S(1)} %collective-permute-done.14, bf16[128,1792]{1,0:T(8,128)(2,1)S(1)} %get-tuple-element.26, bf16[128,1792]{1,0:T(8,128)(2,1)S(1)} %get-tuple-element.24), kind=kOutput, calls=%fused_computation.9 | convolution fusion | flops 3764649984 | bytes 11272192 | tf_op jit(solution)/shard_map/dot_general | solution.py:142
  117.7 1.6 collective-permute-start.5
  121.9 21.8 %collective-permute-done.5 = bf16[512,1024]{1,0:T(8,128)(2,1)S(1)} collective-permute-done((bf16[512,1024]{1,0:T(8,128)(2,1)S(1)}, bf16[512,1024]{1,0:T(8,128)(2,1)S(1)}, u32[]{:S(2)}, u32[]{:S(2)}) %collective-permute-start.5) | collective-permute-done | bytes 1048608 | tf_op jit(solution)/shard_map/ppermute | solution.py:148
  143.7 22.2 %collective-permute-done.16 = bf16[512,1024]{1,0:T(8,128)(2,1)} collective-permute-done((bf16[512,1024]{1,0:T(8,128)(2,1)S(1)}, bf16[512,1024]{1,0:T(8,128)(2,1)}, u32[]{:S(2)}, u32[]{:S(2)}) %collective-permute-start.16) | collective-permute-done | bytes 1048608 | tf_op jit(solution)/shard_map/ppermute | solution.py:148
  165.9 2.2 maximum_convert_fusion.1
  168.7 2.1 collective-permute-done.6
  171.2 4.5 %fusion.22 = bf16[512,896]{1,0:T(8,128)(2,1)S(1)} fusion(bf16[2048,1792]{1,0:T(8,128)(2,1)} %param.10, bf16[512,1024]{1,0:T(8,128)(2,1)S(1)} %get-tuple-element.9, bf16[512,1024]{1,0:T(8,128)(2,1)S(1)} %get-tuple-element.8), kind=kOutput, calls=%fused_computation.39 | convolution fusion | flops 1883701248 | bytes 6684672 | tf_op jit(solution)/shard_map/dot_general | solution.py:157
  175.8 2.3 fusion.28
  178.4 2.3 fusion.31
  180.8 2.3 fusion.25
  183.2 2.0 collective-permute-start.7
  185.4 1.9 collective-permute-start.18
  187.5 9.1 %collective-permute-done.22 = bf16[256,896]{1,0:T(8,128)(2,1)S(1)} collective-permute-done((bf16[256,896]{1,0:T(8,128)(2,1)S(1)}, bf16[256,896]{1,0:T(8,128)(2,1)S(1)}, u32[]{:S(2)}, u32[]{:S(2)}) %collective-permute-start.22) | collective-permute-done | bytes 458784 | tf_op jit(solution)/shard_map/ppermute | solution.py:82
  200.1 6.3 %collective-permute-done.7 = bf16[256,896]{1,0:T(8,128)(2,1)S(1)} collective-permute-done((bf16[256,896]{1,0:T(8,128)(2,1)S(1)}, bf16[256,896]{1,0:T(8,128)(2,1)S(1)}, u32[]{:S(2)}, u32[]{:S(2)}) %collective-permute-start.7) | collective-permute-done | bytes 458784 | tf_op jit(solution)/shard_map/ppermute | solution.py:82
  208.6 7.6 %collective-permute-done.26 = bf16[256,896]{1,0:T(8,128)(2,1)S(1)} collective-permute-done((bf16[256,896]{1,0:T(8,128)(2,1)S(1)}, bf16[256,896]{1,0:T(8,128)(2,1)S(1)}, u32[]{:S(2)}, u32[]{:S(2)}) %collective-permute-start.26) | collective-permute-done | bytes 458784 | tf_op jit(solution)/shard_map/ppermute | solution.py:82
  216.2 1.7 collective-permute-start.8
  218.3 6.9 %collective-permute-done.18 = bf16[256,896]{1,0:T(8,128)(2,1)S(1)} collective-permute-done((bf16[256,896]{1,0:T(8,128)(2,1)S(1)}, bf16[256,896]{1,0:T(8,128)(2,1)S(1)}, u32[]{:S(2)}, u32[]{:S(2)}) %collective-permute-start.18) | collective-permute-done | bytes 458784 | tf_op jit(solution)/shard_map/ppermute | solution.py:82
  227.8 18.4 %collective-permute-done.27 = bf16[256,896]{1,0:T(8,128)(2,1)S(1)} collective-permute-done((bf16[256,896]{1,0:T(8,128)(2,1)S(1)}, bf16[256,896]{1,0:T(8,128)(2,1)S(1)}, u32[]{:S(2)}, u32[]{:S(2)}) %collective-permute-start.27) | collective-permute-done | bytes 458784 | tf_op jit(solution)/shard_map/ppermute | solution.py:70
  246.3 4.4 %collective-permute-start.19 = (bf16[256,896]{1,0:T(8,128)(2,1)S(1)}, bf16[256,896]{1,0:T(8,128)(2,1)S(1)}, u32[]{:S(2)}, u32[]{:S(2)}) collective-permute-start(bf16[256,896]{1,0:T(8,128)(2,1)S(1)} %convolution_convert_fusion.10), channel_id=1, source_target_pairs={{0,8},{4,12},{24,16},{28,20},{1,9},{5,13},{25,17},{29,21},{2,10},{... | collective-permute-start | bytes 1376264 | tf_op jit(solution)/shard_map/ppermute | solution.py:70
  251.6 6.6 %collective-permute-done.19 = bf16[256,896]{1,0:T(8,128)(2,1)S(1)} collective-permute-done((bf16[256,896]{1,0:T(8,128)(2,1)S(1)}, bf16[256,896]{1,0:T(8,128)(2,1)S(1)}, u32[]{:S(2)}, u32[]{:S(2)}) %collective-permute-start.19) | collective-permute-done | bytes 458784 | tf_op jit(solution)/shard_map/ppermute | solution.py:70
  263.5 11.6 %collective-permute-done.29 = bf16[256,896]{1,0:T(8,128)(2,1)S(1)} collective-permute-done((bf16[256,896]{1,0:T(8,128)(2,1)S(1)}, bf16[256,896]{1,0:T(8,128)(2,1)S(1)}, u32[]{:S(2)}, u32[]{:S(2)}) %collective-permute-start.29) | collective-permute-done | bytes 458784 | tf_op jit(solution)/shard_map/ppermute | solution.py:74
  275.3 16.7 %collective-permute-done.21 = bf16[256,896]{1,0:T(8,128)(2,1)S(1)} collective-permute-done((bf16[256,896]{1,0:T(8,128)(2,1)S(1)}, bf16[256,896]{1,0:T(8,128)(2,1)S(1)}, u32[]{:S(2)}, u32[]{:S(2)}) %collective-permute-start.21) | collective-permute-done | bytes 458784 | tf_op jit(solution)/shard_map/ppermute | solution.py:74
  292.8 5.7 %all-reduce = (f32[256]{0:T(256)S(1)}, f32[256]{0:T(256)S(1)}) all-reduce(f32[256]{0:T(256)S(1)} %get-tuple-element.3, f32[256]{0:T(256)S(1)} %get-tuple-element.2), channel_id=1, replica_groups=mesh['lat'=8,'tp'=4] {'tp'}, use_global_device_ids=true, to_apply=%region_2.3 | all-reduce | flops 512 | bytes 4096 | tf_op jit(solution)/shard_map/psum | solution.py:25
  299.7 21.8 %psum.23 = f32[]{:T(128)} all-reduce(f32[]{:T(128)} %get-tuple-element.6), channel_id=1, replica_groups=mesh['lat'=8,'tp'=4] {'lat'}, use_global_device_ids=true, to_apply=%region_6.7 | all-reduce | flops 1 | bytes 8 | tf_op jit(solution)/shard_map/psum | solution.py:29
  (114 shorter events, 32.2 us)
Async XLA Ops:
  2.0 51.5 %collective-permute-start.11 = (bf16[256,1792]{1,0:T(8,128)(2,1)S(1)}, bf16[256,1792]{1,0:T(8,128)(2,1)S(1)}, u32[]{:S(2)}, u32[]{:S(2)}) collective-permute-start(bf16[256,1792]{1,0:T(8,128)(2,1)S(1)} %fusion.8), channel_id=1, source_target_pairs={{0,8},{4,12},{24,16},{28,20},{1,9},{5,13},{25,17},{29,21},{2,10},{... | collective-permute-start | bytes 2752520 | tf_op jit(solution)/shard_map/ppermute | solution.py:70
  7.0 47.3 %collective-permute-start.1 = (bf16[256,1792]{1,0:T(8,128)(2,1)S(1)}, bf16[256,1792]{1,0:T(8,128)(2,1)S(1)}, u32[]{:S(2)}, u32[]{:S(2)}) collective-permute-start(bf16[256,1792]{1,0:T(8,128)(2,1)S(1)} %fusion.8), channel_id=1, source_target_pairs={{8,16},{12,20},{16,8},{20,12},{9,17},{13,21},{17,9},{21,13},{10,18... | collective-permute-start | bytes 2752520 | tf_op jit(solution)/shard_map/ppermute | solution.py:78
  7.7 48.3 %collective-permute-start = (bf16[256,1792]{1,0:T(8,128)(2,1)S(1)}, bf16[256,1792]{1,0:T(8,128)(2,1)}, u32[]{:S(2)}, u32[]{:S(2)}) collective-permute-start(bf16[256,1792]{1,0:T(8,128)(2,1)S(1)} %fusion.8), channel_id=1, source_target_pairs={{8,0},{12,4},{16,24},{20,28},{9,1},{13,5},{17,25},{21,29},{10,2},{... | collective-permute-start | bytes 2752520 | tf_op jit(solution)/shard_map/ppermute | solution.py:74
  53.5 4.3 %collective-permute-start.12 = (bf16[256,1792]{1,0:T(8,128)(2,1)S(1)}, bf16[256,1792]{1,0:T(8,128)(2,1)S(1)}, u32[]{:S(2)}, u32[]{:S(2)}) collective-permute-start(bf16[256,1792]{1,0:T(8,128)(2,1)S(1)} %collective-permute-done.11), channel_id=1, source_target_pairs={{8,16},{12,20},{16,8},{20,12},{9,17},{13,21},{17,9},{21,13},{10,18... | collective-permute-start | bytes 2752520 | tf_op jit(solution)/shard_map/ppermute | solution.py:78
  54.2 24.6 %collective-permute-start.2 = (bf16[256,1792]{1,0:T(8,128)(2,1)S(1)}, bf16[256,1792]{1,0:T(8,128)(2,1)S(1)}, u32[]{:S(2)}, u32[]{:S(2)}) collective-permute-start(bf16[256,1792]{1,0:T(8,128)(2,1)S(1)} %collective-permute-done.1), channel_id=1, source_target_pairs={{8,0},{12,4},{16,24},{20,28},{9,1},{13,5},{17,25},{21,29},{10,2},{... | collective-permute-start | bytes 2752520 | tf_op jit(solution)/shard_map/ppermute | solution.py:74
  57.7 38.4 %slice-start = ((s8[7340032]{0:T(1024)(128)(4,1)}), s8[4194304]{0:T(1024)(128)(4,1)S(1)}, s32[]{:S(2)}) async-start(s8[7340032]{0:T(1024)(128)(4,1)} %bitcast.41), calls=%async_computation | async-start | bytes 8388608
  57.8 34.5 %collective-permute-start.13 = (bf16[256,1792]{1,0:T(8,128)(2,1)S(1)}, bf16[256,1792]{1,0:T(8,128)(2,1)S(1)}, u32[]{:S(2)}, u32[]{:S(2)}) collective-permute-start(bf16[256,1792]{1,0:T(8,128)(2,1)S(1)} %collective-permute-done.12), channel_id=1, source_target_pairs={{8,0},{12,4},{16,24},{20,28},{9,1},{13,5},{17,25},{21,29},{10,2},{... | collective-permute-start | bytes 2752520 | tf_op jit(solution)/shard_map/ppermute | solution.py:74
  79.4 16.7 %collective-permute-start.3 = (bf16[256,1792]{1,0:T(8,128)(2,1)S(1)}, bf16[256,1792]{1,0:T(8,128)(2,1)S(1)}, u32[]{:S(2)}, u32[]{:S(2)}) collective-permute-start(bf16[256,1792]{1,0:T(8,128)(2,1)S(1)} %pad_maximum_fusion.6), channel_id=1, source_target_pairs={{0,4},{4,0},{8,12},{12,8},{16,20},{20,16},{24,28},{28,24},{1,5},{5... | collective-permute-start | bytes 2752520 | tf_op jit(solution)/shard_map/ppermute | solution.py:82
  92.9 19.6 %collective-permute-start.14 = (bf16[256,1792]{1,0:T(8,128)(2,1)S(1)}, bf16[256,1792]{1,0:T(8,128)(2,1)S(1)}, u32[]{:S(2)}, u32[]{:S(2)}) collective-permute-start(bf16[256,1792]{1,0:T(8,128)(2,1)S(1)} %pad_maximum_fusion.7), channel_id=1, source_target_pairs={{0,4},{4,0},{8,12},{12,8},{16,20},{20,16},{24,28},{28,24},{1,5},{5... | collective-permute-start | bytes 2752520 | tf_op jit(solution)/shard_map/ppermute | solution.py:82
  100.3 16.7 %collective-permute-start.4 = (bf16[512,1024]{1,0:T(8,128)(2,1)S(1)}, bf16[512,1024]{1,0:T(8,128)(2,1)S(1)}, u32[]{:S(2)}, u32[]{:S(2)}) collective-permute-start(bf16[512,1024]{1,0:T(8,128)(2,1)S(1)} %broadcast_select_fusion.5), channel_id=1, source_target_pairs={{0,1},{1,0},{2,3},{3,2},{4,5},{5,4},{6,7},{7,6},{8,9},{9,8},{10,11... | collective-permute-start | bytes 3145736 | tf_op jit(solution)/shard_map/ppermute | solution.py:146
  117.0 2.7 collective-permute-start.15
  117.7 26.0 %collective-permute-start.5 = (bf16[512,1024]{1,0:T(8,128)(2,1)S(1)}, bf16[512,1024]{1,0:T(8,128)(2,1)S(1)}, u32[]{:S(2)}, u32[]{:S(2)}) collective-permute-start(bf16[512,1024]{1,0:T(8,128)(2,1)S(1)} %add_convert_fusion.1), channel_id=1, source_target_pairs={{0,2},{1,3},{2,0},{3,1},{4,6},{5,7},{6,4},{7,5},{8,10},{9,11},{10,... | collective-permute-start | bytes 3145736 | tf_op jit(solution)/shard_map/ppermute | solution.py:148
  120.3 45.6 %collective-permute-start.16 = (bf16[512,1024]{1,0:T(8,128)(2,1)S(1)}, bf16[512,1024]{1,0:T(8,128)(2,1)}, u32[]{:S(2)}, u32[]{:S(2)}) collective-permute-start(bf16[512,1024]{1,0:T(8,128)(2,1)S(1)} %add_convert_fusion), channel_id=1, source_target_pairs={{0,2},{1,3},{2,0},{3,1},{4,6},{5,7},{6,4},{7,5},{8,10},{9,11},{10,... | collective-permute-start | bytes 3145736 | tf_op jit(solution)/shard_map/ppermute | solution.py:148
  168.2 2.7 collective-permute-start.6
  168.2 10.0 %collective-permute-start.17 = (bf16[512,1024]{1,0:T(8,128)(2,1)S(1)}, bf16[512,1024]{1,0:T(8,128)(2,1)S(1)}, u32[]{:S(2)}, u32[]{:S(2)}) collective-permute-start(bf16[512,1024]{1,0:T(8,128)(2,1)S(1)} %get-tuple-element.41), channel_id=1, source_target_pairs={{0,1},{1,0},{2,3},{3,2},{4,5},{5,4},{6,7},{7,6},{8,9},{9,8},{10,11... | collective-permute-start | bytes 3145736 | tf_op jit(solution)/shard_map/ppermute | solution.py:151
  183.1 13.4 %collective-permute-start.22 = (bf16[256,896]{1,0:T(8,128)(2,1)S(1)}, bf16[256,896]{1,0:T(8,128)(2,1)S(1)}, u32[]{:S(2)}, u32[]{:S(2)}) collective-permute-start(bf16[256,896]{1,0:T(8,128)(2,1)S(1)} %slice.193), channel_id=1, source_target_pairs={{0,4},{4,0},{8,12},{12,8},{16,20},{20,16},{24,28},{28,24},{1,5},{5... | collective-permute-start | bytes 1376264 | tf_op jit(solution)/shard_map/ppermute | solution.py:82
  183.2 23.2 %collective-permute-start.7 = (bf16[256,896]{1,0:T(8,128)(2,1)S(1)}, bf16[256,896]{1,0:T(8,128)(2,1)S(1)}, u32[]{:S(2)}, u32[]{:S(2)}) collective-permute-start(bf16[256,896]{1,0:T(8,128)(2,1)S(1)} %slice.175), channel_id=1, source_target_pairs={{0,4},{4,0},{8,12},{12,8},{16,20},{20,16},{24,28},{28,24},{1,5},{5... | collective-permute-start | bytes 1376264 | tf_op jit(solution)/shard_map/ppermute | solution.py:82
  185.3 30.9 %collective-permute-start.26 = (bf16[256,896]{1,0:T(8,128)(2,1)S(1)}, bf16[256,896]{1,0:T(8,128)(2,1)S(1)}, u32[]{:S(2)}, u32[]{:S(2)}) collective-permute-start(bf16[256,896]{1,0:T(8,128)(2,1)S(1)} %slice.198), channel_id=1, source_target_pairs={{0,4},{4,0},{8,12},{12,8},{16,20},{20,16},{24,28},{28,24},{1,5},{5... | collective-permute-start | bytes 1376264 | tf_op jit(solution)/shard_map/ppermute | solution.py:82
  185.4 39.8 %collective-permute-start.18 = (bf16[256,896]{1,0:T(8,128)(2,1)S(1)}, bf16[256,896]{1,0:T(8,128)(2,1)S(1)}, u32[]{:S(2)}, u32[]{:S(2)}) collective-permute-start(bf16[256,896]{1,0:T(8,128)(2,1)S(1)} %slice.188), channel_id=1, source_target_pairs={{0,4},{4,0},{8,12},{12,8},{16,20},{20,16},{24,28},{28,24},{1,5},{5... | collective-permute-start | bytes 1376264 | tf_op jit(solution)/shard_map/ppermute | solution.py:82
  196.9 65.2 %collective-permute-start.25 = (bf16[256,896]{1,0:T(8,128)(2,1)S(1)}, bf16[256,896]{1,0:T(8,128)(2,1)S(1)}, u32[]{:S(2)}, u32[]{:S(2)}) collective-permute-start(bf16[256,896]{1,0:T(8,128)(2,1)S(1)} %convolution_convert_fusion.9), channel_id=1, source_target_pairs={{0,8},{4,12},{24,16},{28,20},{1,9},{5,13},{25,17},{29,21},{2,10},{... | collective-permute-start | bytes 1376264 | tf_op jit(solution)/shard_map/ppermute | solution.py:70
  198.8 52.0 %collective-permute-start.23 = (bf16[256,896]{1,0:T(8,128)(2,1)S(1)}, bf16[256,896]{1,0:T(8,128)(2,1)S(1)}, u32[]{:S(2)}, u32[]{:S(2)}) collective-permute-start(bf16[256,896]{1,0:T(8,128)(2,1)S(1)} %convolution_convert_fusion.8), channel_id=1, source_target_pairs={{0,8},{4,12},{24,16},{28,20},{1,9},{5,13},{25,17},{29,21},{2,10},{... | collective-permute-start | bytes 1376264 | tf_op jit(solution)/shard_map/ppermute | solution.py:70
  206.8 68.6 %collective-permute-start.10 = (bf16[256,896]{1,0:T(8,128)(2,1)S(1)}, bf16[256,896]{1,0:T(8,128)(2,1)S(1)}, u32[]{:S(2)}, u32[]{:S(2)}) collective-permute-start(bf16[256,896]{1,0:T(8,128)(2,1)S(1)} %convolution_convert_fusion.13), channel_id=1, source_target_pairs={{0,8},{4,12},{24,16},{28,20},{1,9},{5,13},{25,17},{29,21},{2,10},{... | collective-permute-start | bytes 1376264 | tf_op jit(solution)/shard_map/ppermute | solution.py:70
  216.2 43.7 %collective-permute-start.8 = (bf16[256,896]{1,0:T(8,128)(2,1)S(1)}, bf16[256,896]{1,0:T(8,128)(2,1)S(1)}, u32[]{:S(2)}, u32[]{:S(2)}) collective-permute-start(bf16[256,896]{1,0:T(8,128)(2,1)S(1)} %convolution_convert_fusion.12), channel_id=1, source_target_pairs={{0,8},{4,12},{24,16},{28,20},{1,9},{5,13},{25,17},{29,21},{2,10},{... | collective-permute-start | bytes 1376264 | tf_op jit(solution)/shard_map/ppermute | solution.py:70
  225.2 21.0 %collective-permute-start.27 = (bf16[256,896]{1,0:T(8,128)(2,1)S(1)}, bf16[256,896]{1,0:T(8,128)(2,1)S(1)}, u32[]{:S(2)}, u32[]{:S(2)}) collective-permute-start(bf16[256,896]{1,0:T(8,128)(2,1)S(1)} %convolution_convert_fusion.6), channel_id=1, source_target_pairs={{0,8},{4,12},{24,16},{28,20},{1,9},{5,13},{25,17},{29,21},{2,10},{... | collective-permute-start | bytes 1376264 | tf_op jit(solution)/shard_map/ppermute | solution.py:70
  246.3 12.0 %collective-permute-start.19 = (bf16[256,896]{1,0:T(8,128)(2,1)S(1)}, bf16[256,896]{1,0:T(8,128)(2,1)S(1)}, u32[]{:S(2)}, u32[]{:S(2)}) collective-permute-start(bf16[256,896]{1,0:T(8,128)(2,1)S(1)} %convolution_convert_fusion.10), channel_id=1, source_target_pairs={{0,8},{4,12},{24,16},{28,20},{1,9},{5,13},{25,17},{29,21},{2,10},{... | collective-permute-start | bytes 1376264 | tf_op jit(solution)/shard_map/ppermute | solution.py:70
  250.8 8.3 %collective-permute-start.28 = (bf16[256,896]{1,0:T(8,128)(2,1)S(1)}, bf16[256,896]{1,0:T(8,128)(2,1)S(1)}, u32[]{:S(2)}, u32[]{:S(2)}) collective-permute-start(bf16[256,896]{1,0:T(8,128)(2,1)S(1)} %add_convert_fusion.3), channel_id=1, source_target_pairs={{8,16},{12,20},{16,8},{20,12},{9,17},{13,21},{17,9},{21,13},{10,18... | collective-permute-start | bytes 1376264 | tf_op jit(solution)/shard_map/ppermute | solution.py:78
  258.3 5.2 %collective-permute-start.24 = (bf16[256,896]{1,0:T(8,128)(2,1)S(1)}, bf16[256,896]{1,0:T(8,128)(2,1)S(1)}, u32[]{:S(2)}, u32[]{:S(2)}) collective-permute-start(bf16[256,896]{1,0:T(8,128)(2,1)S(1)} %add_convert_fusion.4), channel_id=1, source_target_pairs={{8,16},{12,20},{16,8},{20,12},{9,17},{13,21},{17,9},{21,13},{10,18... | collective-permute-start | bytes 1376264 | tf_op jit(solution)/shard_map/ppermute | solution.py:78
  259.1 2.2 collective-permute-start.20
  259.9 15.2 %collective-permute-start.29 = (bf16[256,896]{1,0:T(8,128)(2,1)S(1)}, bf16[256,896]{1,0:T(8,128)(2,1)S(1)}, u32[]{:S(2)}, u32[]{:S(2)}) collective-permute-start(bf16[256,896]{1,0:T(8,128)(2,1)S(1)} %add_convert_fusion.2), channel_id=1, source_target_pairs={{8,0},{12,4},{16,24},{20,28},{9,1},{13,5},{17,25},{21,29},{10,2},{... | collective-permute-start | bytes 1376264 | tf_op jit(solution)/shard_map/ppermute | solution.py:74
  261.3 14.0 %collective-permute-start.9 = (bf16[256,896]{1,0:T(8,128)(2,1)S(1)}, bf16[256,896]{1,0:T(8,128)(2,1)S(1)}, u32[]{:S(2)}, u32[]{:S(2)}) collective-permute-start(bf16[256,896]{1,0:T(8,128)(2,1)S(1)} %add_convert_fusion.7), channel_id=1, source_target_pairs={{8,16},{12,20},{16,8},{20,12},{9,17},{13,21},{17,9},{21,13},{10,18... | collective-permute-start | bytes 1376264 | tf_op jit(solution)/shard_map/ppermute | solution.py:78
  262.2 29.9 %collective-permute-start.21 = (bf16[256,896]{1,0:T(8,128)(2,1)S(1)}, bf16[256,896]{1,0:T(8,128)(2,1)S(1)}, u32[]{:S(2)}, u32[]{:S(2)}) collective-permute-start(bf16[256,896]{1,0:T(8,128)(2,1)S(1)} %add_convert_fusion.5), channel_id=1, source_target_pairs={{8,0},{12,4},{16,24},{20,28},{9,1},{13,5},{17,25},{21,29},{10,2},{... | collective-permute-start | bytes 1376264 | tf_op jit(solution)/shard_map/ppermute | solution.py:74
  275.3 17.0 %copy-start = (bf16[256,1792]{1,0:T(8,128)(2,1)S(1)}, bf16[256,1792]{1,0:T(8,128)(2,1)}, u32[]{:S(2)}) copy-start(bf16[256,1792]{1,0:T(8,128)(2,1)} %param.6) | copy-start | bytes 2752516
  (5 other events, 47.4 us)

commit v2 on v0

--- a/solution.py
+++ b/solution.py
@@ -1,6 +1,10 @@
+import functools
+
 import jax
 import jax.numpy as jnp
 from jax import lax
+from jax.experimental import pallas as pl
+from jax.experimental.pallas import tpu as pltpu
 from jax.sharding import PartitionSpec as P
 
 
@@ -17,7 +21,21 @@
     return lax.all_to_all(decoded, "lat", split_axis=0, concat_axis=0, tiled=True)
 
 
-def body(activations, active_blocks, enc_weight, enc_bias, dec_weight, dec_bias):
+def finish(activations, summed, dec_bias, owners):
+    token_count = activations.shape[0]
+    recon = summed + dec_bias
+    inputs_full = activations.astype(jnp.float32)
+    diff = inputs_full - recon
+    squares, norms = lax.psum(
+        (jnp.sum(diff * diff, axis=1), jnp.sum(inputs_full * inputs_full, axis=1)), "tp"
+    )
+    token_error = squares / (norms + 1e-06)
+    total = lax.psum(jnp.sum(token_error), "lat")
+    mean_error = total / (token_count * owners)
+    return (token_error, mean_error)
+
+
+def general_body(activations, active_blocks, enc_weight, enc_bias, dec_weight, dec_bias):
     owners = lax.axis_size("lat")
     token_count, active_count = active_blocks.shape
     feature_part = activations.shape[1]
@@ -36,19 +54,446 @@
     returned = score_slots(received, enc_weight, enc_bias, dec_weight)
     returned = returned.reshape(owners * capacity, feature_part)
     picked = returned[slot_rows].reshape(token_count, active_count, feature_part)
-    recon = jnp.sum(picked.astype(jnp.float32), axis=1) + dec_bias
-    inputs_full = activations.astype(jnp.float32)
-    diff = inputs_full - recon
-    squares, norms = lax.psum(
-        (jnp.sum(diff * diff, axis=1), jnp.sum(inputs_full * inputs_full, axis=1)), "tp"
-    )
-    token_error = squares / (norms + 1e-06)
-    total = lax.psum(jnp.sum(token_error), "lat")
-    mean_error = total / (token_count * owners)
-    return (token_error, mean_error)
+    return finish(activations, jnp.sum(picked.astype(jnp.float32), axis=1), dec_bias, owners)
+
+
+MESH = pl.DeviceIdType.MESH
+TILE = 256
+ROW_PARTS = 4
+
+
+def line_kernel(
+    tokens, capacity,
+    act, blocks, enc_hbm, enc_bias, dec_hbm, dec_bias,
+    error_out, mean_out,
+    enc, dec, src, meta, picks, places, rows, ysend, given, other, kept, chip, side, lat,
+    theirs, cat, part, from_mate, from_far, from_end, across2, across3,
+    acc, norm, stats, stats_in, mean_own, mean_in,
+    w_sem, hop_send, hop_recv, meta_send, meta_recv, pair_send, pair_recv,
+    back_send, back_recv, sum_send, sum_recv, end_send, end_recv,
+):
+    me, tp = lax.axis_index("lat"), lax.axis_index("tp")
+    plane, column = me // 2, me % 2
+    core = tp % 2
+    inner = ((plane + 1) // 2) % 2 == 1
+    outer = ((plane + 1) // 2) % 2 == 0
+    width = act.shape[1]
+    tiles = width // TILE
+    half = enc.shape[1] // 2
+    part_rows = tokens // ROW_PARTS
+
+    def flip(value, mask):
+        for bit in (1, 2, 4):
+            if mask & bit:
+                value = value + bit - 2 * bit * ((value // bit) % 2)
+        return value
+
+    def lat_peer(mask):
+        return (flip(me, mask), tp)
+
+    def tp_peer(mask):
+        return (me, flip(tp, mask))
+
+    MATE, ACROSS, OPPOSITE, COLUMN = 2, 6, 4, 1
+
+    def remote(src_ref, dst_ref, send, recv, peer):
+        return pltpu.make_async_remote_copy(
+            src_ref=src_ref, dst_ref=dst_ref, send_sem=send, recv_sem=recv,
+            device_id=peer, device_id_type=MESH,
+        )
+
+    enc_copy = pltpu.make_async_copy(enc_hbm, enc, w_sem.at[0])
+    dec_copy = pltpu.make_async_copy(dec_hbm, dec, w_sem.at[1])
+    enc_copy.start()
+    dec_copy.start()
+
+    def centre(t, carry):
+        cols = pl.ds(pl.multiple_of(t * TILE, TILE), TILE)
+        src[0, :, cols] = (act[:, cols].astype(jnp.float32) - dec_bias[:, cols]).astype(jnp.bfloat16)
+        return carry
+
+    lax.fori_loop(0, tiles, centre, 0)
+    meta[0] = blocks[...]
+
+    barrier = pltpu.get_barrier_semaphore()
+    for mask in range(1, 8):
+        pl.semaphore_signal(barrier, inc=1, device_id=lat_peer(mask), device_id_type=MESH)
+    for mask in range(1, 4):
+        pl.semaphore_signal(barrier, inc=1, device_id=tp_peer(mask), device_id_type=MESH)
+    pl.semaphore_wait(barrier, 10)
+
+    far_slot = 3 - ((plane + 1) // 2) % 2
+    meta_copies = [
+        remote(meta.at[0], meta.at[1], meta_send.at[0], meta_recv.at[1], lat_peer(MATE)),
+        remote(meta.at[0], meta.at[far_slot], meta_send.at[1], meta_recv.at[far_slot], lat_peer(ACROSS)),
+        remote(meta.at[0], meta.at[far_slot], meta_send.at[2], meta_recv.at[far_slot], lat_peer(OPPOSITE)),
+    ]
+    for copy in meta_copies:
+        copy.start()
+
+    flows = [(0, 1, MATE), (0, 2, ACROSS), (2, 2, MATE), (1, 3, ACROSS), (3, 3, MATE)]
+
+    def hop(flow, piece):
+        here, there, mask = flows[flow]
+        span = pl.ds(pl.multiple_of(piece * part_rows, part_rows), part_rows)
+        return remote(
+            src.at[here, span], src.at[there, span],
+            hop_send.at[flow, piece], hop_recv.at[there, piece], lat_peer(mask),
+        )
+
+    def each_piece(fn):
+        lax.fori_loop(0, ROW_PARTS, lambda c, carry: (fn(c), carry)[1], 0)
+
+    def each_tile(fn):
+        lax.fori_loop(0, tiles, lambda t, carry: (fn(t), carry)[1], 0)
+
+    each_piece(lambda c: hop(0, c).start())
+
+    @pl.when(inner)
+    def _():
+        each_piece(lambda c: hop(1, c).start())
+
+    def squares_of_inputs(t):
+        cols = pl.ds(pl.multiple_of(t * TILE, TILE), TILE)
+        value = act[:, cols].astype(jnp.float32)
+        norm[...] += value * value
+
+    norm[...] = jnp.zeros_like(norm)
+    acc[...] = jnp.zeros_like(acc)
+    each_tile(squares_of_inputs)
+
+    earlier = (
+        lax.broadcasted_iota(jnp.int32, (tokens, tokens), 0)
+        < lax.broadcasted_iota(jnp.int32, (tokens, tokens), 1)
+    ).astype(jnp.float32).astype(jnp.bfloat16)
+    slots = lax.broadcasted_iota(jnp.int32, (capacity, tokens), 0).astype(jnp.float32)
+
+    def make_picks(k):
+        names = meta[k]
+        named = []
+        for owner in (me, flip(me, COLUMN)):
+            hit = jnp.max((names == owner).astype(jnp.float32), axis=0, keepdims=True)
+            named.append(jnp.broadcast_to(hit, (8, tokens)))
+        named = jnp.concatenate(named)
+        ranks = jnp.dot(named.astype(jnp.bfloat16), earlier, preferred_element_type=jnp.float32)
+        pick = jnp.concatenate([
+            jnp.where(ranks[8 * i:8 * i + 1] == slots, named[8 * i:8 * i + 1], 0.0)
+            for i in range(2)
+        ])
+        picks[k] = pick.astype(jnp.bfloat16)
+        places[k] = pick.T.astype(jnp.bfloat16)
+
+    def to_column(k):
+        return remote(
+            ysend.at[k], rows.at[k, pl.ds(capacity, capacity)],
+            pair_send.at[0, k], pair_recv.at[0, k], lat_peer(COLUMN),
+        )
+
+    def to_core(k):
+        return remote(given.at[k], other.at[k], pair_send.at[1, k], pair_recv.at[1, k], tp_peer(1))
+
+    def to_side(k):
+        return remote(chip.at[k], side.at[k], pair_send.at[2, k], pair_recv.at[2, k], tp_peer(2))
+
+    def to_core2(k):
+        return remote(
+            lat.at[k, core], lat.at[k, core], pair_send.at[3, k], pair_recv.at[3, k], tp_peer(1)
+        )
+
+    def pick_rows(k):
+        make_picks(k)
+
+        def tile(t):
+            cols = pl.ds(pl.multiple_of(t * TILE, TILE), TILE)
+            got = jnp.dot(picks[k], src[k, :, cols], preferred_element_type=jnp.float32)
+            got = got.astype(jnp.bfloat16)
+            rows[k, pl.ds(0, capacity), cols] = got[:capacity]
+            ysend[k, :, cols] = got[capacity:]
+
+        each_tile(tile)
+        to_column(k).start()
+
+    def encode(k):
+        to_column(k).wait_recv()
+
+        def into(target, first):
+            def tile(t, carry):
+                cols = pl.ds(pl.multiple_of(first + t * TILE, TILE), TILE)
+                value = jnp.dot(rows[k], enc[:, cols], preferred_element_type=jnp.float32)
+                target(pl.ds(pl.multiple_of(t * TILE, TILE), TILE), value.astype(jnp.bfloat16))
+                return carry
+
+            lax.fori_loop(0, half // TILE, tile, 0)
+
+        def set_given(cols, value):
+            given[k, :, cols] = value
+
+        def set_kept(cols, value):
+            kept[:, cols] = value
+
+        into(set_given, (1 - core) * half)
+        to_core(k).start()
+        into(set_kept, core * half)
+        to_core(k).wait_recv()
+        chip[k] = (kept[...].astype(jnp.float32) + other[k].astype(jnp.float32)).astype(jnp.bfloat16)
+        to_side(k).start()
+
+    def activate(k):
+        to_side(k).wait_recv()
+        bias = enc_bias[:, pl.ds(pl.multiple_of(core * half, half), half)]
+        pre = chip[k].astype(jnp.float32) + side[k].astype(jnp.float32) + bias
+        lat[k, core] = jnp.maximum(pre, 0.0).astype(jnp.bfloat16)
+        to_core2(k).start()
+
+    def back(k, t):
+        return remote(
+            theirs.at[k, t], cat.at[k, t, pl.ds(capacity, capacity)],
+            back_send.at[k, t], back_recv.at[k, t], lat_peer(COLUMN),
+        )
+
+    def decode(k):
+        to_core2(k).wait_recv()
+
+        def tile(t):
+            cols = pl.ds(pl.multiple_of(t * TILE, TILE), TILE)
+            value = jnp.dot(lat[k, 0], dec[pl.ds(0, half), cols], preferred_element_type=jnp.float32)
+            value += jnp.dot(lat[k, 1], dec[pl.ds(half, half), cols], preferred_element_type=jnp.float32)
+            value = value.astype(jnp.bfloat16)
+            cat[k, t, pl.ds(0, capacity)] = value[:capacity]
+            theirs[k, t] = value[capacity:]
+            back(k, t).start()
+
+        each_tile(tile)
+
+    sums = [(1, from_mate, MATE), (2, from_far, MATE), (3, from_end, MATE), (2, across2, ACROSS), (3, across3, ACROSS)]
+
+    def pass_on(flow, t):
+        k, target, mask = sums[flow]
+        return remote(
+            part.at[k, t], target.at[t], sum_send.at[flow, t], sum_recv.at[flow, t], lat_peer(mask)
+        )
+
+    def add_to_part(k, t, more):
+        part[k, t] = (part[k, t].astype(jnp.float32) + more[t].astype(jnp.float32)).astype(jnp.bfloat16)
+
+    def place(k):
+        def tile(t):
+            back(k, t).wait_recv()
+            value = jnp.dot(places[k], cat[k, t], preferred_element_type=jnp.float32)
+            part[k, t] = value.astype(jnp.bfloat16)
+            if k >= 1:
+                @pl.when(outer)
+                def _():
+                    pass_on(k - 1, t).start()
+
+            if k >= 2:
+                @pl.when(inner)
+                def _():
+                    pass_on(k - 1, t).wait_recv()
+                    add_to_part(k, t, (None, None, from_far, from_end)[k])
+                    pass_on(k + 1, t).start()
+
+        each_tile(tile)
+
+    def wait_slot(k):
+        each_piece(lambda c: hop((0, 0, 1, 3)[k], c).wait_recv())
+
+    meta_done = [
+        remote(meta.at[0], meta.at[k], meta_send.at[0], meta_recv.at[k], lat_peer(MATE))
+        for k in range(1, 4)
+    ]
+
+    pick_rows(0)
+    enc_copy.wait()
+    encode(0)
+
+    @pl.when(inner)
+    def _():
+        def forward_far(c):
+            hop(1, c).wait_recv()
+            hop(2, c).start()
+
+        def forward_mate(c):
+            hop(0, c).wait_recv()
+            hop(3, c).start()
+
+        each_piece(forward_far)
+        each_piece(forward_mate)
+
+    @pl.when(outer)
+    def _():
+        wait_slot(1)
+
+    meta_done[0].wait_recv()
+    pick_rows(1)
+    encode(1)
+    activate(0)
+
+    @pl.when(outer)
+    def _():
+        wait_slot(2)
+
+    meta_done[1].wait_recv()
+    pick_rows(2)
+
+    @pl.when(inner)
+    def _():
+        def forward_end(c):
+            hop(3, c).wait_recv()
+            hop(4, c).start()
+
+        each_piece(forward_end)
+
+    encode(2)
+    dec_copy.wait()
+    activate(1)
+    decode(0)
+    decode(1)
+    place(0)
+    place(1)
+
+    @pl.when(outer)
+    def _():
+        wait_slot(3)
+
+    meta_done[2].wait_recv()
+    pick_rows(3)
+    encode(3)
+    activate(2)
+    decode(2)
+    place(2)
+    activate(3)
+    decode(3)
+    place(3)
+
+    @pl.when(inner)
+    def _():
+        def tile(t):
+            pass_on(4, t).wait_recv()
+            add_to_part(1, t, across3)
+            pass_on(0, t).start()
+
+        each_tile(tile)
+
+    def finish_tile(t):
+        pass_on(0, t).wait_recv()
+        cols = pl.ds(pl.multiple_of(t * TILE, TILE), TILE)
+        diff = act[:, cols].astype(jnp.float32) - dec_bias[:, cols]
+        diff = diff - part[0, t].astype(jnp.float32) - from_mate[t].astype(jnp.float32)
+        return diff
+
+    @pl.when(outer)
+    def _():
+        def tile(t):
+            diff = finish_tile(t)
+            acc[...] += diff * diff
+
+        each_tile(tile)
+
+    @pl.when(inner)
+    def _():
+        def tile(t):
+            pass_on(3, t).wait_recv()
+            diff = finish_tile(t) - across2[t].astype(jnp.float32)
+            acc[...] += diff * diff
+
+        each_tile(tile)
+
+    stats[0:1] = jnp.sum(acc[...].T, axis=0, keepdims=True)
+    stats[1:2] = jnp.sum(norm[...].T, axis=0, keepdims=True)
+    stats[2:8] = jnp.zeros((6, tokens), jnp.float32)
+    stat_copies = [
+        remote(stats, stats_in.at[m], end_send.at[m], end_recv.at[m], tp_peer(m)) for m in range(1, 4)
+    ]
+    for copy in stat_copies:
+        copy.start()
+    for copy in stat_copies:
+        copy.wait()
+    both = (stats[...] + stats_in[1]) + (stats_in[2] + stats_in[3])
+    error = both[0:1] / (both[1:2] + 1e-06)
+    error_out[...] = jnp.broadcast_to(error, (8, tokens))
+    mean_own[...] = jnp.broadcast_to(jnp.sum(error, axis=1, keepdims=True), (8, 128))
+    mean_copies = [
+        remote(mean_own, mean_in.at[m], end_send.at[3 + m], end_recv.at[3 + m], lat_peer(m))
+        for m in range(1, 8)
+    ]
+    for copy in mean_copies:
+        copy.start()
+    for copy in mean_copies:
+        copy.wait()
+    low = (mean_own[...] + mean_in[1]) + (mean_in[2] + mean_in[3])
+    high = (mean_in[4] + mean_in[5]) + (mean_in[6] + mean_in[7])
+    mean_out[...] = (low + high) / (tokens * 8)
+
+    for copy in meta_copies:
+        copy.wait_send()
+    each_piece(lambda c: hop(0, c).wait_send())
+    for k in range(4):
+        for copy in (to_column(k), to_core(k), to_side(k), to_core2(k)):
+            copy.wait_send()
+        each_tile(lambda t: back(k, t).wait_send())
+    each_tile(lambda t: pass_on(0, t).wait_send())
+
+    @pl.when(inner)
+    def _():
+        for flow in range(1, 5):
+            each_piece(lambda c: hop(flow, c).wait_send())
+        for flow in (3, 4):
+            each_tile(lambda t: pass_on(flow, t).wait_send())
+
+    @pl.when(outer)
+    def _():
+        for flow in (1, 2):
+            each_tile(lambda t: pass_on(flow, t).wait_send())
+
+
+def line_body(activations, active_blocks, enc_weight, enc_bias, dec_weight, dec_bias):
+    tokens, active_count = active_blocks.shape
+    capacity = 2 * tokens * active_count // 8
+    width = activations.shape[1]
+    block = enc_weight.shape[1]
+    half = block // 2
+    tiles = width // TILE
+    names = jnp.pad(active_blocks.T, ((0, 8 - active_count), (0, 0)), constant_values=-1)
+    bf, f32 = jnp.bfloat16, jnp.float32
+    vm, dma = pltpu.VMEM, pltpu.SemaphoreType.DMA
+    in_vmem = pl.BlockSpec(memory_space=pltpu.VMEM)
+    anywhere = pl.BlockSpec(memory_space=pl.ANY)
+    tiled = (tiles, tokens, TILE)
+    error, mean = pl.pallas_call(
+        functools.partial(line_kernel, tokens, capacity),
+        out_shape=(jax.ShapeDtypeStruct((8, tokens), f32), jax.ShapeDtypeStruct((8, 128), f32)),
+        in_specs=[in_vmem, in_vmem, anywhere, in_vmem, anywhere, in_vmem],
+        out_specs=(in_vmem, in_vmem),
+        scratch_shapes=[
+            vm((width, block), bf), vm((block, width), bf),
+            vm((4, tokens, width), bf), vm((4, 8, tokens), jnp.int32),
+            vm((4, 2 * capacity, tokens), bf), vm((4, tokens, 2 * capacity), bf),
+            vm((4, 2 * capacity, width), bf), vm((4, capacity, width), bf),
+            vm((4, 2 * capacity, half), bf), vm((4, 2 * capacity, half), bf),
+            vm((2 * capacity, half), bf), vm((4, 2 * capacity, half), bf),
+            vm((4, 2 * capacity, half), bf), vm((4, 2, 2 * capacity, half), bf),
+            vm((4, tiles, capacity, TILE), bf), vm((4, tiles, 2 * capacity, TILE), bf),
+            vm((4,) + tiled, bf),
+            vm(tiled, bf), vm(tiled, bf), vm(tiled, bf), vm(tiled, bf), vm(tiled, bf),
+            vm((tokens, TILE), f32), vm((tokens, TILE), f32),
+            vm((8, tokens), f32), vm((4, 8, tokens), f32), vm((8, 128), f32), vm((8, 8, 128), f32),
+            dma((2,)), dma((5, ROW_PARTS)), dma((4, ROW_PARTS)), dma((3,)), dma((4,)),
+            dma((4, 4)), dma((4, 4)), dma((4, tiles)), dma((4, tiles)),
+            dma((5, tiles)), dma((5, tiles)), dma((11,)), dma((11,)),
+        ],
+        compiler_params=pltpu.CompilerParams(
+            collective_id=0, has_side_effects=True, vmem_limit_bytes=60 * 1024 * 1024
+        ),
+        cost_estimate=pl.CostEstimate(
+            flops=4 * 8 * capacity * width * block, bytes_accessed=4 * width * block, transcendentals=0
+        ),
+    )(activations, names, enc_weight, enc_bias[None], dec_weight, dec_bias[None])
+    return error[0], mean[0, 0]
 
 
 def solution(mesh):
     in_specs = (P("lat", "tp"), P("lat", None), P("tp", "lat"), P("lat"), P("lat", "tp"), P("tp"))
     out_specs = (P("lat"), P())
+    body = line_body if (mesh.shape["lat"], mesh.shape["tp"]) == (8, 4) else general_body
     return jax.shard_map(body, mesh=mesh, in_specs=in_specs, out_specs=out_specs, check_vma=False)

time: 360 us -> 187 us (0.52)
  Pallas kernels: 0 us -> 181 us
  waiting for transfers between devices: 167 us -> 0 us
  blocking collectives: 116 us -> 0 us
  matrix products: 24.3 us -> 0 us
  local copies, waits for them, and re-layouts: 20.3 us -> 5.01 us
  between operations: 15.9 us -> 0.64 us
  other arithmetic: 11.4 us -> 0 us
  starting transfers between devices: 5.55 us -> 0 us
    pallas_call x0 -> x1, Pallas kernels: none -> 181 us  [line_body(): pl.pallas_call(functools.partial(line_kernel, tokens, capacity), out_shap...]
    all_to_all x1 -> x0, blocking collectives: 89.2 us -> none  [body(): lax.all_to_all(outgoing, 'lat', split_axis=0, concat_axis=0, tiled=True)]
    psum x1 -> x0, waiting for transfers between devices: 84.7 us -> none  [score_slots(): pre = lax.psum(partial_value.astype(jnp.bfloat16), 'tp').astype(jnp.float32)]
    all_to_all x1 -> x0, waiting for transfers between devices: 81.9 us -> none  [score_slots(): lax.all_to_all(decoded, 'lat', split_axis=0, concat_axis=0, tiled=True)]
    psum x2 -> x0, blocking collectives: 26.5 us -> none  [the longest x1 20.8 us: body(): total = lax.psum(jnp.sum(token_error), 'lat')]
    dot_general x2 -> x0, matrix products: 24.3 us -> none  [the longest x1 12.9 us: score_slots(): jnp.dot(latents, dec_weight, preferred_element_type=jnp.float32)]
    reduce_sum x4 -> x0, other arithmetic: 8.22 us -> none  [the longest x1 6.46 us: body(): recon = jnp.sum(picked.astype(jnp.float32), axis=1) + dec_bias]
    scatter x1 -> x0, local copies, waits for them, and re-layouts: 6.58 us -> none  [body(): jnp.zeros((owners * capacity, feature_part), jnp.bfloat16).at[slot_rows]]
  transfers between devices with their start and end apart: 2 -> 0, of which waited for: 2 -> 0; matrix products, arithmetic and copies ran while one was open for 0% -> 0% of each run, Pallas kernels for 0% -> 0%
where the time goes in v2:
time: 187 us; the launch traced here: 186 us
  Pallas kernels  181 us (97%)
  local copies, waits for them, and re-layouts  5.01 us (3%)
    pallas_call x1, Pallas kernels, line_body(): pl.pallas_call(functools.partial(line_kernel, tokens, capacity), out_shap...  181 us

profile of v2, /device:TPU:0, one launch (start us, length us, event | category | flops | bytes accessed | tf_op | source)
XLA Modules:
  0.0 186.5 jit_solution(9140735581616473173)
XLA Ops:
  0.6 1.3 broadcast_in_dim.7.dec_bias
  1.9 1.3 pad.4.blocks
  3.2 180.8 %shard_map.77 = (f32[8,256]{1,0:T(8,128)}, f32[8,128]{1,0:T(8,128)}) custom-call(bf16[256,1792]{1,0:T(8,128)(2,1)} %act.1, s32[8,256]{1,0:T(8,128)} %pad.4.blocks, bf16[1792,2048]{1,0:T(8,128)(2,1)} %enc_hbm.1, f32[1,2048]{1,0:T(1,128)} %bitcast.6, bf16[2048,1792]{1,0:T(8,128)(2,1)} %dec_hbm.1, f32[1,1792]{1,0:T(1,128)} %broadcast_in_dim.7.dec_bias), custom_call_target="tpu_custom_call" | custom-call | flops 15032385536 | bytes 14680064 | tf_op jit(solution)/shard_map/pallas_call | solution.py:463
  184.0 1.2 slice.7
  185.2 1.3 slice.6

commit v3 on v2

--- a/solution.py
+++ b/solution.py
@@ -59,17 +59,16 @@
 
 MESH = pl.DeviceIdType.MESH
 TILE = 256
-ROW_PARTS = 4
 
 
 def line_kernel(
     tokens, capacity,
     act, blocks, enc_hbm, enc_bias, dec_hbm, dec_bias,
     error_out, mean_out,
-    enc, dec, src, meta, picks, places, rows, ysend, given, other, kept, chip, side, lat,
+    enc, dec, src, meta, picks, places, rows, ysend, given, other, chip, side, lat,
     theirs, cat, part, from_mate, from_far, from_end, across2, across3,
     acc, norm, stats, stats_in, mean_own, mean_in,
-    w_sem, hop_send, hop_recv, meta_send, meta_recv, pair_send, pair_recv,
+    w_sem, hop_send, hop_recv, meta_send, meta_recv, col_send, col_recv, pair_send, pair_recv,
     back_send, back_recv, sum_send, sum_recv, end_send, end_recv,
 ):
     me, tp = lax.axis_index("lat"), lax.axis_index("tp")
@@ -80,7 +79,7 @@
     width = act.shape[1]
     tiles = width // TILE
     half = enc.shape[1] // 2
-    part_rows = tokens // ROW_PARTS
+    half_tiles = half // TILE
 
     def flip(value, mask):
         for bit in (1, 2, 4):
@@ -95,6 +94,9 @@
         return (me, flip(tp, mask))
 
     MATE, ACROSS, OPPOSITE, COLUMN = 2, 6, 4, 1
+
+    def columns(t, first=0):
+        return pl.ds(pl.multiple_of(first + t * TILE, TILE), TILE)
 
     def remote(src_ref, dst_ref, send, recv, peer):
         return pltpu.make_async_remote_copy(
@@ -135,23 +137,22 @@
 
     def hop(flow, piece):
         here, there, mask = flows[flow]
-        span = pl.ds(pl.multiple_of(piece * part_rows, part_rows), part_rows)
-        return remote(
-            src.at[here, span], src.at[there, span],
+        return remote(
+            src.at[here, :, columns(piece)], src.at[there, :, columns(piece)],
             hop_send.at[flow, piece], hop_recv.at[there, piece], lat_peer(mask),
         )
-
-    def each_piece(fn):
-        lax.fori_loop(0, ROW_PARTS, lambda c, carry: (fn(c), carry)[1], 0)
 
     def each_tile(fn):
         lax.fori_loop(0, tiles, lambda t, carry: (fn(t), carry)[1], 0)
 
-    each_piece(lambda c: hop(0, c).start())
+    def each_half_tile(fn):
+        lax.fori_loop(0, half_tiles, lambda t, carry: (fn(t), carry)[1], 0)
+
+    each_tile(lambda t: hop(0, t).start())
 
     @pl.when(inner)
     def _():
-        each_piece(lambda c: hop(1, c).start())
+        each_tile(lambda t: hop(1, t).start())
 
     def squares_of_inputs(t):
         cols = pl.ds(pl.multiple_of(t * TILE, TILE), TILE)
@@ -183,67 +184,66 @@
         picks[k] = pick.astype(jnp.bfloat16)
         places[k] = pick.T.astype(jnp.bfloat16)
 
-    def to_column(k):
-        return remote(
-            ysend.at[k], rows.at[k, pl.ds(capacity, capacity)],
-            pair_send.at[0, k], pair_recv.at[0, k], lat_peer(COLUMN),
-        )
-
-    def to_core(k):
-        return remote(given.at[k], other.at[k], pair_send.at[1, k], pair_recv.at[1, k], tp_peer(1))
-
-    def to_side(k):
-        return remote(chip.at[k], side.at[k], pair_send.at[2, k], pair_recv.at[2, k], tp_peer(2))
-
-    def to_core2(k):
-        return remote(
-            lat.at[k, core], lat.at[k, core], pair_send.at[3, k], pair_recv.at[3, k], tp_peer(1)
-        )
-
-    def pick_rows(k):
-        make_picks(k)
-
-        def tile(t):
-            cols = pl.ds(pl.multiple_of(t * TILE, TILE), TILE)
-            got = jnp.dot(picks[k], src[k, :, cols], preferred_element_type=jnp.float32)
-            got = got.astype(jnp.bfloat16)
-            rows[k, pl.ds(0, capacity), cols] = got[:capacity]
-            ysend[k, :, cols] = got[capacity:]
-
-        each_tile(tile)
-        to_column(k).start()
+    def to_column(k, t):
+        return remote(
+            ysend.at[k, :, columns(t)], rows.at[k, pl.ds(capacity, capacity), columns(t)],
+            col_send.at[k, t], col_recv.at[k, t], lat_peer(COLUMN),
+        )
+
+    def to_core(k, t):
+        return remote(
+            given.at[k, :, columns(t)], other.at[k, :, columns(t)],
+            pair_send.at[0, k, t], pair_recv.at[0, k, t], tp_peer(1),
+        )
+
+    def to_side(k, t):
+        return remote(
+            chip.at[k, :, columns(t)], side.at[k, :, columns(t)],
+            pair_send.at[1, k, t], pair_recv.at[1, k, t], tp_peer(2),
+        )
+
+    def to_core2(k, t):
+        return remote(
+            lat.at[k, core, :, columns(t)], lat.at[k, core, :, columns(t)],
+            pair_send.at[2, k, t], pair_recv.at[2, k, t], tp_peer(1),
+        )
+
+    def pick_tile(k, t):
+        got = jnp.dot(picks[k], src[k, :, columns(t)], preferred_element_type=jnp.float32)
+        got = got.astype(jnp.bfloat16)
+        rows[k, pl.ds(0, capacity), columns(t)] = got[:capacity]
+        ysend[k, :, columns(t)] = got[capacity:]
+        to_column(k, t).start()
 
     def encode(k):
-        to_column(k).wait_recv()
-
-        def into(target, first):
-            def tile(t, carry):
-                cols = pl.ds(pl.multiple_of(first + t * TILE, TILE), TILE)
-                value = jnp.dot(rows[k], enc[:, cols], preferred_element_type=jnp.float32)
-                target(pl.ds(pl.multiple_of(t * TILE, TILE), TILE), value.astype(jnp.bfloat16))
-                return carry
-
-            lax.fori_loop(0, half // TILE, tile, 0)
-
-        def set_given(cols, value):
-            given[k, :, cols] = value
-
-        def set_kept(cols, value):
-            kept[:, cols] = value
-
-        into(set_given, (1 - core) * half)
-        to_core(k).start()
-        into(set_kept, core * half)
-        to_core(k).wait_recv()
-        chip[k] = (kept[...].astype(jnp.float32) + other[k].astype(jnp.float32)).astype(jnp.bfloat16)
-        to_side(k).start()
+        each_tile(lambda t: to_column(k, t).wait_recv())
+
+        def give(t):
+            cols = columns(t, (1 - core) * half)
+            value = jnp.dot(rows[k], enc[:, cols], preferred_element_type=jnp.float32)
+            given[k, :, columns(t)] = value.astype(jnp.bfloat16)
+            to_core(k, t).start()
+
+        def keep(t):
+            cols = columns(t, core * half)
+            value = jnp.dot(rows[k], enc[:, cols], preferred_element_type=jnp.float32)
+            to_core(k, t).wait_recv()
+            value += other[k, :, columns(t)].astype(jnp.float32)
+            chip[k, :, columns(t)] = value.astype(jnp.bfloat16)
+            to_side(k, t).start()
+
+        each_half_tile(give)
+        each_half_tile(keep)
 
     def activate(k):
-        to_side(k).wait_recv()
-        bias = enc_bias[:, pl.ds(pl.multiple_of(core * half, half), half)]
-        pre = chip[k].astype(jnp.float32) + side[k].astype(jnp.float32) + bias
-        lat[k, core] = jnp.maximum(pre, 0.0).astype(jnp.bfloat16)
-        to_core2(k).start()
+        def tile(t):
+            to_side(k, t).wait_recv()
+            bias = enc_bias[:, columns(t, core * half)]
+            pre = chip[k, :, columns(t)].astype(jnp.float32) + side[k, :, columns(t)].astype(jnp.float32)
+            lat[k, core, :, columns(t)] = jnp.maximum(pre + bias, 0.0).astype(jnp.bfloat16)
+            to_core2(k, t).start()
+
+        each_half_tile(tile)
 
     def back(k, t):
         return remote(
@@ -252,7 +252,7 @@
         )
 
     def decode(k):
-        to_core2(k).wait_recv()
+        each_half_tile(lambda t: to_core2(k, t).wait_recv())
 
         def tile(t):
             cols = pl.ds(pl.multiple_of(t * TILE, TILE), TILE)
@@ -276,104 +276,123 @@
     def add_to_part(k, t, more):
         part[k, t] = (part[k, t].astype(jnp.float32) + more[t].astype(jnp.float32)).astype(jnp.bfloat16)
 
+    def place_tile(k, t):
+        back(k, t).wait_recv()
+        value = jnp.dot(places[k], cat[k, t], preferred_element_type=jnp.float32)
+        part[k, t] = value.astype(jnp.bfloat16)
+        if k >= 1:
+            @pl.when(outer)
+            def _():
+                pass_on(k - 1, t).start()
+
     def place(k):
-        def tile(t):
-            back(k, t).wait_recv()
-            value = jnp.dot(places[k], cat[k, t], preferred_element_type=jnp.float32)
-            part[k, t] = value.astype(jnp.bfloat16)
-            if k >= 1:
-                @pl.when(outer)
-                def _():
-                    pass_on(k - 1, t).start()
-
-            if k >= 2:
-                @pl.when(inner)
-                def _():
-                    pass_on(k - 1, t).wait_recv()
-                    add_to_part(k, t, (None, None, from_far, from_end)[k])
-                    pass_on(k + 1, t).start()
-
-        each_tile(tile)
-
-    def wait_slot(k):
-        each_piece(lambda c: hop((0, 0, 1, 3)[k], c).wait_recv())
+        each_tile(lambda t: place_tile(k, t))
 
     meta_done = [
         remote(meta.at[0], meta.at[k], meta_send.at[0], meta_recv.at[k], lat_peer(MATE))
         for k in range(1, 4)
     ]
 
-    pick_rows(0)
+    make_picks(0)
+    each_tile(lambda t: pick_tile(0, t))
+    for k in range(1, 4):
+        meta_done[k - 1].wait_recv()
+        make_picks(k)
+
+    @pl.when(inner)
+    def _():
+        def tile(t):
+            hop(1, t).wait_recv()
+            hop(2, t).start()
+            hop(0, t).wait_recv()
+            hop(3, t).start()
+            pick_tile(1, t)
+
+        each_tile(tile)
+
+    @pl.when(outer)
+    def _():
+        def tile(t):
+            hop(0, t).wait_recv()
+            pick_tile(1, t)
+
+        each_tile(tile)
+
     enc_copy.wait()
     encode(0)
+    encode(1)
 
     @pl.when(inner)
     def _():
-        def forward_far(c):
-            hop(1, c).wait_recv()
-            hop(2, c).start()
-
-        def forward_mate(c):
-            hop(0, c).wait_recv()
-            hop(3, c).start()
-
-        each_piece(forward_far)
-        each_piece(forward_mate)
+        def tile(t):
+            hop(3, t).wait_recv()
+            hop(4, t).start()
+            pick_tile(3, t)
+
+        each_tile(lambda t: pick_tile(2, t))
+        each_tile(tile)
 
     @pl.when(outer)
     def _():
-        wait_slot(1)
-
-    meta_done[0].wait_recv()
-    pick_rows(1)
-    encode(1)
+        def tile(t):
+            hop(2, t).wait_recv()
+            pick_tile(2, t)
+
+        each_tile(tile)
+
     activate(0)
-
-    @pl.when(outer)
-    def _():
-        wait_slot(2)
-
-    meta_done[1].wait_recv()
-    pick_rows(2)
-
-    @pl.when(inner)
-    def _():
-        def forward_end(c):
-            hop(3, c).wait_recv()
-            hop(4, c).start()
-
-        each_piece(forward_end)
-
     encode(2)
+    activate(1)
     dec_copy.wait()
-    activate(1)
     decode(0)
     decode(1)
-    place(0)
-    place(1)
 
     @pl.when(outer)
     def _():
-        wait_slot(3)
-
-    meta_done[2].wait_recv()
-    pick_rows(3)
+        def tile(t):
+            hop(3, t).wait_recv()
+            pick_tile(3, t)
+
+        each_tile(tile)
+
     encode(3)
     activate(2)
     decode(2)
+    place(1)
     place(2)
     activate(3)
     decode(3)
-    place(3)
+    place(0)
+
+    @pl.when(outer)
+    def _():
+        place(3)
 
     @pl.when(inner)
     def _():
-        def tile(t):
+        def far_tile(t):
+            pass_on(1, t).wait_recv()
+            add_to_part(2, t, from_far)
+            pass_on(3, t).start()
+
+        def last_hop(t):
             pass_on(4, t).wait_recv()
             add_to_part(1, t, across3)
             pass_on(0, t).start()
 
-        each_tile(tile)
+        def end_tile(t):
+            place_tile(3, t)
+            pass_on(2, t).wait_recv()
+            add_to_part(3, t, from_end)
+            pass_on(4, t).start()
+
+            @pl.when(t >= 1)
+            def _():
+                last_hop(t - 1)
+
+        each_tile(far_tile)
+        each_tile(end_tile)
+        last_hop(tiles - 1)
 
     def finish_tile(t):
         pass_on(0, t).wait_recv()
@@ -427,17 +446,18 @@
 
     for copy in meta_copies:
         copy.wait_send()
-    each_piece(lambda c: hop(0, c).wait_send())
+    each_tile(lambda t: hop(0, t).wait_send())
     for k in range(4):
-        for copy in (to_column(k), to_core(k), to_side(k), to_core2(k)):
-            copy.wait_send()
+        each_tile(lambda t: to_column(k, t).wait_send())
+        for flow in (to_core, to_side, to_core2):
+            each_half_tile(lambda t: flow(k, t).wait_send())
         each_tile(lambda t: back(k, t).wait_send())
     each_tile(lambda t: pass_on(0, t).wait_send())
 
     @pl.when(inner)
     def _():
         for flow in range(1, 5):
-            each_piece(lambda c: hop(flow, c).wait_send())
+            each_tile(lambda t: hop(flow, t).wait_send())
         for flow in (3, 4):
             each_tile(lambda t: pass_on(flow, t).wait_send())
 
@@ -471,15 +491,16 @@
             vm((4, 2 * capacity, tokens), bf), vm((4, tokens, 2 * capacity), bf),
             vm((4, 2 * capacity, width), bf), vm((4, capacity, width), bf),
             vm((4, 2 * capacity, half), bf), vm((4, 2 * capacity, half), bf),
-            vm((2 * capacity, half), bf), vm((4, 2 * capacity, half), bf),
-            vm((4, 2 * capacity, half), bf), vm((4, 2, 2 * capacity, half), bf),
+            vm((4, 2 * capacity, half), bf), vm((4, 2 * capacity, half), bf),
+            vm((4, 2, 2 * capacity, half), bf),
             vm((4, tiles, capacity, TILE), bf), vm((4, tiles, 2 * capacity, TILE), bf),
             vm((4,) + tiled, bf),
             vm(tiled, bf), vm(tiled, bf), vm(tiled, bf), vm(tiled, bf), vm(tiled, bf),
             vm((tokens, TILE), f32), vm((tokens, TILE), f32),
             vm((8, tokens), f32), vm((4, 8, tokens), f32), vm((8, 128), f32), vm((8, 8, 128), f32),
-            dma((2,)), dma((5, ROW_PARTS)), dma((4, ROW_PARTS)), dma((3,)), dma((4,)),
-            dma((4, 4)), dma((4, 4)), dma((4, tiles)), dma((4, tiles)),
+            dma((2,)), dma((5, tiles)), dma((4, tiles)), dma((3,)), dma((4,)),
+            dma((4, tiles)), dma((4, tiles)), dma((3, 4, half // TILE)), dma((3, 4, half // TILE)),
+            dma((4, tiles)), dma((4, tiles)),
             dma((5, tiles)), dma((5, tiles)), dma((11,)), dma((11,)),
         ],
         compiler_params=pltpu.CompilerParams(

time: 187 us -> 186 us (level)
  no operation moved by 1% of the time
where the time goes in v3:
time: 186 us
  Pallas kernels  180 us (97%)
  local copies, waits for them, and re-layouts  5.01 us (3%)
    pallas_call x1, Pallas kernels, line_body(): pl.pallas_call(functools.partial(line_kernel, tokens, capacity), out_shap...  180 us

profile of v3, /device:TPU:0, one launch (start us, length us, event | category | flops | bytes accessed | tf_op | source)
XLA Modules:
  0.0 185.6 jit_solution(17732388185319588405)
XLA Ops:
  0.6 1.3 broadcast_in_dim.7.dec_bias
  1.9 1.3 pad.4.blocks
  3.2 180.0 %shard_map.77 = (f32[8,256]{1,0:T(8,128)}, f32[8,128]{1,0:T(8,128)}) custom-call(bf16[256,1792]{1,0:T(8,128)(2,1)} %act.1, s32[8,256]{1,0:T(8,128)} %pad.4.blocks, bf16[1792,2048]{1,0:T(8,128)(2,1)} %enc_hbm.1, f32[1,2048]{1,0:T(1,128)} %bitcast.6, bf16[2048,1792]{1,0:T(8,128)(2,1)} %dec_hbm.1, f32[1,1792]{1,0:T(1,128)} %broadcast_in_dim.7.dec_bias), custom_call_target="tpu_custom_call" | custom-call | flops 15032385536 | bytes 14680064 | tf_op jit(solution)/shard_map/pallas_call | solution.py:483
  183.2 1.2 slice.7
  184.4 1.3 slice.6

commit v4 on v3

--- a/solution.py
+++ b/solution.py
@@ -142,17 +142,20 @@
             hop_send.at[flow, piece], hop_recv.at[there, piece], lat_peer(mask),
         )
 
-    def each_tile(fn):
-        lax.fori_loop(0, tiles, lambda t, carry: (fn(t), carry)[1], 0)
+    def each_tile(fn, first=0, last=tiles):
+        lax.fori_loop(first, last, lambda t, carry: (fn(t), carry)[1], 0)
 
     def each_half_tile(fn):
         lax.fori_loop(0, half_tiles, lambda t, carry: (fn(t), carry)[1], 0)
 
-    each_tile(lambda t: hop(0, t).start())
-
-    @pl.when(inner)
-    def _():
-        each_tile(lambda t: hop(1, t).start())
+    def first_hops(t):
+        hop(0, t).start()
+
+        @pl.when(inner)
+        def _():
+            hop(1, t).start()
+
+    each_tile(first_hops)
 
     def squares_of_inputs(t):
         cols = pl.ds(pl.multiple_of(t * TILE, TILE), TILE)
@@ -251,19 +254,17 @@
             back_send.at[k, t], back_recv.at[k, t], lat_peer(COLUMN),
         )
 
-    def decode(k):
+    def wait_latents(k):
         each_half_tile(lambda t: to_core2(k, t).wait_recv())
 
-        def tile(t):
-            cols = pl.ds(pl.multiple_of(t * TILE, TILE), TILE)
-            value = jnp.dot(lat[k, 0], dec[pl.ds(0, half), cols], preferred_element_type=jnp.float32)
-            value += jnp.dot(lat[k, 1], dec[pl.ds(half, half), cols], preferred_element_type=jnp.float32)
-            value = value.astype(jnp.bfloat16)
-            cat[k, t, pl.ds(0, capacity)] = value[:capacity]
-            theirs[k, t] = value[capacity:]
-            back(k, t).start()
-
-        each_tile(tile)
+    def decode_tile(k, t):
+        cols = columns(t)
+        value = jnp.dot(lat[k, 0], dec[pl.ds(0, half), cols], preferred_element_type=jnp.float32)
+        value += jnp.dot(lat[k, 1], dec[pl.ds(half, half), cols], preferred_element_type=jnp.float32)
+        value = value.astype(jnp.bfloat16)
+        cat[k, t, pl.ds(0, capacity)] = value[:capacity]
+        theirs[k, t] = value[capacity:]
+        back(k, t).start()
 
     sums = [(1, from_mate, MATE), (2, from_far, MATE), (3, from_end, MATE), (2, across2, ACROSS), (3, across3, ACROSS)]
 
@@ -285,8 +286,15 @@
             def _():
                 pass_on(k - 1, t).start()
 
-    def place(k):
-        each_tile(lambda t: place_tile(k, t))
+    LAG = 3
+
+    def place_behind(k, t):
+        @pl.when(t >= LAG)
+        def _():
+            place_tile(k, t - LAG)
+
+    def place_rest(k):
+        each_tile(lambda t: place_tile(k, t), tiles - LAG)
 
     meta_done = [
         remote(meta.at[0], meta.at[k], meta_send.at[0], meta_recv.at[k], lat_peer(MATE))
@@ -299,74 +307,80 @@
         meta_done[k - 1].wait_recv()
         make_picks(k)
 
-    @pl.when(inner)
-    def _():
-        def tile(t):
+    def mate_arrives(t):
+        @pl.when(inner)
+        def _():
             hop(1, t).wait_recv()
             hop(2, t).start()
-            hop(0, t).wait_recv()
+
+        hop(0, t).wait_recv()
+
+        @pl.when(inner)
+        def _():
             hop(3, t).start()
-            pick_tile(1, t)
-
-        each_tile(tile)
+
+        pick_tile(1, t)
+
+    def far_inner_arrives(t):
+        @pl.when(outer)
+        def _():
+            hop(2, t).wait_recv()
+
+        @pl.when(inner)
+        def _():
+            hop(3, t).wait_recv()
+            hop(4, t).start()
+
+        pick_tile(2, t)
+        decode_tile(0, t)
+
+    def far_outer_arrives(t):
+        @pl.when(outer)
+        def _():
+            hop(3, t).wait_recv()
+
+        pick_tile(3, t)
+        decode_tile(1, t)
+        place_behind(1, t)
+
+    def third_decode(t):
+        decode_tile(2, t)
+        place_behind(2, t)
+        place_tile(0, t)
+
+    def last_decode(t):
+        decode_tile(3, t)
+
+        @pl.when(outer)
+        def _():
+            place_behind(3, t)
+
+    each_tile(mate_arrives, 0, tiles // 2)
+    enc_copy.wait()
+    encode(0)
+    each_tile(mate_arrives, tiles // 2, tiles)
+    encode(1)
+    activate(0)
+    dec_copy.wait()
+    wait_latents(0)
+    each_tile(far_inner_arrives)
+    activate(1)
+    encode(2)
+    wait_latents(1)
+    each_tile(far_outer_arrives)
+    activate(2)
+    place_rest(1)
+    encode(3)
+    wait_latents(2)
+    each_tile(third_decode)
+    place_rest(2)
+    activate(3)
+    wait_latents(3)
+    each_tile(last_decode)
 
     @pl.when(outer)
     def _():
-        def tile(t):
-            hop(0, t).wait_recv()
-            pick_tile(1, t)
-
-        each_tile(tile)
-
-    enc_copy.wait()
-    encode(0)
-    encode(1)
-
-    @pl.when(inner)
-    def _():
-        def tile(t):
-            hop(3, t).wait_recv()
-            hop(4, t).start()
-            pick_tile(3, t)
-
-        each_tile(lambda t: pick_tile(2, t))
-        each_tile(tile)
-
-    @pl.when(outer)
-    def _():
-        def tile(t):
-            hop(2, t).wait_recv()
-            pick_tile(2, t)
-
-        each_tile(tile)
-
-    activate(0)
-    encode(2)
-    activate(1)
-    dec_copy.wait()
-    decode(0)
-    decode(1)
-
-    @pl.when(outer)
-    def _():
-        def tile(t):
-            hop(3, t).wait_recv()
-            pick_tile(3, t)
-
-        each_tile(tile)
-
-    encode(3)
-    activate(2)
-    decode(2)
-    place(1)
-    place(2)
-    activate(3)
-    decode(3)
-    place(0)
-
-    @pl.when(outer)
-    def _():
-        place(3)
+        place_rest(3)
 
     @pl.when(inner)
     def _():

time: 186 us -> 171 us (0.919)
  Pallas kernels: 180 us -> 165 us
    pallas_call x1, Pallas kernels: 180 us -> 165 us  [line_body(): pl.pallas_call(functools.partial(line_kernel, tokens, capacity), out_shap...]
where the time goes in v4:
time: 171 us; the launch traced here: 170 us
  Pallas kernels  165 us (96%)
  local copies, waits for them, and re-layouts  5.01 us (3%)
    pallas_call x1, Pallas kernels, line_body(): pl.pallas_call(functools.partial(line_kernel, tokens, capacity), out_shap...  165 us

profile of v4, /device:TPU:0, one launch (start us, length us, event | category | flops | bytes accessed | tf_op | source)
XLA Modules:
  0.0 170.2 jit_solution(12484374884422583586)
XLA Ops:
  0.6 1.3 broadcast_in_dim.7.dec_bias
  1.9 1.3 pad.4.blocks
  3.2 164.5 %shard_map.77 = (f32[8,256]{1,0:T(8,128)}, f32[8,128]{1,0:T(8,128)}) custom-call(bf16[256,1792]{1,0:T(8,128)(2,1)} %act.1, s32[8,256]{1,0:T(8,128)} %pad.4.blocks, bf16[1792,2048]{1,0:T(8,128)(2,1)} %enc_hbm.1, f32[1,2048]{1,0:T(1,128)} %bitcast.6, bf16[2048,1792]{1,0:T(8,128)(2,1)} %dec_hbm.1, f32[1,1792]{1,0:T(1,128)} %broadcast_in_dim.7.dec_bias), custom_call_target="tpu_custom_call" | custom-call | flops 15032385536 | bytes 14680064 | tf_op jit(solution)/shard_map/pallas_call | solution.py:497
  167.7 1.2 slice.7
  168.9 1.3 slice.6

commit v5 on v4

--- a/solution.py
+++ b/solution.py
@@ -111,11 +111,13 @@
 
     def centre(t, carry):
         cols = pl.ds(pl.multiple_of(t * TILE, TILE), TILE)
-        src[0, :, cols] = (act[:, cols].astype(jnp.float32) - dec_bias[:, cols]).astype(jnp.bfloat16)
+        src[0, :, cols] = (act[:, cols].astype(jnp.float32) - dec_bias[cols][None]).astype(jnp.bfloat16)
         return carry
 
     lax.fori_loop(0, tiles, centre, 0)
-    meta[0] = blocks[...]
+    active_count = blocks.shape[0]
+    meta[0, 0:active_count] = blocks[...]
+    meta[0, active_count:8] = jnp.full((8 - active_count, tokens), -1, jnp.int32)
 
     barrier = pltpu.get_barrier_semaphore()
     for mask in range(1, 8):
@@ -241,7 +243,7 @@
     def activate(k):
         def tile(t):
             to_side(k, t).wait_recv()
-            bias = enc_bias[:, columns(t, core * half)]
+            bias = enc_bias[columns(t, core * half)][None]
             pre = chip[k, :, columns(t)].astype(jnp.float32) + side[k, :, columns(t)].astype(jnp.float32)
             lat[k, core, :, columns(t)] = jnp.maximum(pre + bias, 0.0).astype(jnp.bfloat16)
             to_core2(k, t).start()
@@ -264,7 +266,8 @@
         value = value.astype(jnp.bfloat16)
         cat[k, t, pl.ds(0, capacity)] = value[:capacity]
         theirs[k, t] = value[capacity:]
-        back(k, t).start()
+        if k >= 1:
+            back(k, t).start()
 
     sums = [(1, from_mate, MATE), (2, from_far, MATE), (3, from_end, MATE), (2, across2, ACROSS), (3, across3, ACROSS)]
 
@@ -340,13 +343,11 @@
             hop(3, t).wait_recv()
 
         pick_tile(3, t)
-        decode_tile(1, t)
-        place_behind(1, t)
+        place_tile(1, t)
 
     def third_decode(t):
         decode_tile(2, t)
         place_behind(2, t)
-        place_tile(0, t)
 
     def last_decode(t):
         decode_tile(3, t)
@@ -363,13 +364,14 @@
     activate(0)
     dec_copy.wait()
     wait_latents(0)
-    each_tile(far_inner_arrives)
+    each_tile(far_inner_arrives, 0, tiles - 2)
     activate(1)
+    each_tile(far_inner_arrives, tiles - 2, tiles)
+    wait_latents(1)
+    each_tile(lambda t: decode_tile(1, t))
     encode(2)
-    wait_latents(1)
     each_tile(far_outer_arrives)
     activate(2)
-    place_rest(1)
     encode(3)
     wait_latents(2)
     each_tile(third_decode)
@@ -377,10 +379,12 @@
     activate(3)
     wait_latents(3)
     each_tile(last_decode)
+    each_tile(lambda t: back(0, t).start())
 
     @pl.when(outer)
     def _():
         place_rest(3)
+        each_tile(lambda t: place_tile(0, t))
 
     @pl.when(inner)
     def _():
@@ -388,6 +392,7 @@
             pass_on(1, t).wait_recv()
             add_to_part(2, t, from_far)
             pass_on(3, t).start()
+            place_tile(0, t)
 
         def last_hop(t):
             pass_on(4, t).wait_recv()
@@ -411,7 +416,7 @@
     def finish_tile(t):
         pass_on(0, t).wait_recv()
         cols = pl.ds(pl.multiple_of(t * TILE, TILE), TILE)
-        diff = act[:, cols].astype(jnp.float32) - dec_bias[:, cols]
+        diff = act[:, cols].astype(jnp.float32) - dec_bias[cols][None]
         diff = diff - part[0, t].astype(jnp.float32) - from_mate[t].astype(jnp.float32)
         return diff
 
@@ -444,7 +449,7 @@
         copy.wait()
     both = (stats[...] + stats_in[1]) + (stats_in[2] + stats_in[3])
     error = both[0:1] / (both[1:2] + 1e-06)
-    error_out[...] = jnp.broadcast_to(error, (8, tokens))
+    error_out[...] = error[0]
     mean_own[...] = jnp.broadcast_to(jnp.sum(error, axis=1, keepdims=True), (8, 128))
     mean_copies = [
         remote(mean_own, mean_in.at[m], end_send.at[3 + m], end_recv.at[3 + m], lat_peer(m))
@@ -456,7 +461,7 @@
         copy.wait()
     low = (mean_own[...] + mean_in[1]) + (mean_in[2] + mean_in[3])
     high = (mean_in[4] + mean_in[5]) + (mean_in[6] + mean_in[7])
-    mean_out[...] = (low + high) / (tokens * 8)
+    mean_out[0, 0] = jnp.max((low + high) / (tokens * 8))
 
     for copy in meta_copies:
         copy.wait_send()
@@ -488,7 +493,6 @@
     block = enc_weight.shape[1]
     half = block // 2
     tiles = width // TILE
-    names = jnp.pad(active_blocks.T, ((0, 8 - active_count), (0, 0)), constant_values=-1)
     bf, f32 = jnp.bfloat16, jnp.float32
     vm, dma = pltpu.VMEM, pltpu.SemaphoreType.DMA
     in_vmem = pl.BlockSpec(memory_space=pltpu.VMEM)
@@ -496,9 +500,9 @@
     tiled = (tiles, tokens, TILE)
     error, mean = pl.pallas_call(
         functools.partial(line_kernel, tokens, capacity),
-        out_shape=(jax.ShapeDtypeStruct((8, tokens), f32), jax.ShapeDtypeStruct((8, 128), f32)),
+        out_shape=(jax.ShapeDtypeStruct((tokens,), f32), jax.ShapeDtypeStruct((1, 1), f32)),
         in_specs=[in_vmem, in_vmem, anywhere, in_vmem, anywhere, in_vmem],
-        out_specs=(in_vmem, in_vmem),
+        out_specs=(in_vmem, pl.BlockSpec(memory_space=pltpu.SMEM)),
         scratch_shapes=[
             vm((width, block), bf), vm((block, width), bf),
             vm((4, tokens, width), bf), vm((4, 8, tokens), jnp.int32),
@@ -523,8 +527,8 @@
         cost_estimate=pl.CostEstimate(
             flops=4 * 8 * capacity * width * block, bytes_accessed=4 * width * block, transcendentals=0
         ),
-    )(activations, names, enc_weight, enc_bias[None], dec_weight, dec_bias[None])
-    return error[0], mean[0, 0]
+    )(activations, active_blocks.T, enc_weight, enc_bias, dec_weight, dec_bias)
+    return error, mean[0, 0]
 
 
 def solution(mesh):

time: 171 us -> 163 us (0.953)
  Pallas kernels: 165 us -> 159 us
  local copies, waits for them, and re-layouts: 5.01 us -> 1.22 us
  between operations: 0.64 us -> 2.4 us
    pallas_call x1, Pallas kernels: 165 us -> 159 us  [line_body(): pl.pallas_call(functools.partial(line_kernel, tokens, capacity), out_shap...]
    slice x2 -> x0, local copies, waits for them, and re-layouts: 2.44 us -> none  [line_body(): return (error[0], mean[0, 0])]
where the time goes in v5:
time: 163 us
  Pallas kernels  159 us (98%)
  between operations  2.4 us (1%)
    pallas_call x1, Pallas kernels, line_body(): pl.pallas_call(functools.partial(line_kernel, tokens, capacity), out_shap...  159 us

profile of v5, /device:TPU:0, one launch (start us, length us, event | category | flops | bytes accessed | tf_op | source)
XLA Modules:
  0.0 162.6 jit_solution(8581934745504207756)
XLA Ops:
  0.6 159.0 %shard_map.77 = (f32[256]{0:T(256)}, f32[1,1]{1,0:T(1,128)}) custom-call(bf16[256,1792]{1,0:T(8,128)(2,1)} %act.1, s32[2,256]{1,0:T(2,128)} %bitcast.2, bf16[1792,2048]{1,0:T(8,128)(2,1)} %enc_hbm.1, f32[2048]{0:T(1024)} %enc_bias.1, bf16[2048,1792]{1,0:T(8,128)(2,1)} %dec_hbm.1, f32[1792]{0:T(1024)} %dec_bias.1), custom_call_target="tpu_custom_call" | custom-call | flops 15032385536 | bytes 14680064 | tf_op jit(solution)/shard_map/pallas_call | solution.py:501
  159.6 1.2 copy.10

commit v6 on v5

--- a/solution.py
+++ b/solution.py
@@ -335,7 +335,10 @@
             hop(4, t).start()
 
         pick_tile(2, t)
-        decode_tile(0, t)
+
+        @pl.when(inner)
+        def _():
+            decode_tile(0, t)
 
     def far_outer_arrives(t):
         @pl.when(outer)
@@ -343,7 +346,10 @@
             hop(3, t).wait_recv()
 
         pick_tile(3, t)
-        place_tile(1, t)
+
+    def second_decode(t):
+        decode_tile(1, t)
+        place_behind(1, t)
 
     def third_decode(t):
         decode_tile(2, t)
@@ -364,12 +370,12 @@
     activate(0)
     dec_copy.wait()
     wait_latents(0)
-    each_tile(far_inner_arrives, 0, tiles - 2)
+    each_tile(far_inner_arrives)
     activate(1)
-    each_tile(far_inner_arrives, tiles - 2, tiles)
     wait_latents(1)
-    each_tile(lambda t: decode_tile(1, t))
+    each_tile(second_decode)
     encode(2)
+    place_rest(1)
     each_tile(far_outer_arrives)
     activate(2)
     encode(3)
@@ -379,11 +385,15 @@
     activate(3)
     wait_latents(3)
     each_tile(last_decode)
-    each_tile(lambda t: back(0, t).start())
 
     @pl.when(outer)
     def _():
+        def own_decode(t):
+            decode_tile(0, t)
+            back(0, t).start()
+
         place_rest(3)
+        each_tile(own_decode)
         each_tile(lambda t: place_tile(0, t))
 
     @pl.when(inner)
@@ -409,6 +419,7 @@
             def _():
                 last_hop(t - 1)
 
+        each_tile(lambda t: back(0, t).start())
         each_tile(far_tile)
         each_tile(end_tile)
         last_hop(tiles - 1)

time: 163 us -> 167 us (1.025)
  Pallas kernels: 159 us -> 163 us
    pallas_call x1, Pallas kernels: 159 us -> 163 us  [line_body(): pl.pallas_call(functools.partial(line_kernel, tokens, capacity), out_shap...]
where the time goes in v6:
time: 167 us
  Pallas kernels  163 us (98%)
  between operations  2.4 us (1%)
    pallas_call x1, Pallas kernels, line_body(): pl.pallas_call(functools.partial(line_kernel, tokens, capacity), out_shap...  163 us

profile of v6, /device:TPU:0, one launch (start us, length us, event | category | flops | bytes accessed | tf_op | source)
XLA Modules:
  0.0 166.6 jit_solution(4370458366314253910)
XLA Ops:
  0.6 163.0 %shard_map.77 = (f32[256]{0:T(256)}, f32[1,1]{1,0:T(1,128)}) custom-call(bf16[256,1792]{1,0:T(8,128)(2,1)} %act.1, s32[2,256]{1,0:T(2,128)} %bitcast.2, bf16[1792,2048]{1,0:T(8,128)(2,1)} %enc_hbm.1, f32[2048]{0:T(1024)} %enc_bias.1, bf16[2048,1792]{1,0:T(8,128)(2,1)} %dec_hbm.1, f32[1792]{0:T(1024)} %dec_bias.1), custom_call_target="tpu_custom_call" | custom-call | flops 15032385536 | bytes 14680064 | tf_op jit(solution)/shard_map/pallas_call | solution.py:512
  163.6 1.2 copy.10

commit v7 on v5

--- a/solution.py
+++ b/solution.py
@@ -343,7 +343,10 @@
             hop(3, t).wait_recv()
 
         pick_tile(3, t)
-        place_tile(1, t)
+
+    def second_decode(t):
+        decode_tile(1, t)
+        place_behind(1, t)
 
     def third_decode(t):
         decode_tile(2, t)
@@ -368,8 +371,9 @@
     activate(1)
     each_tile(far_inner_arrives, tiles - 2, tiles)
     wait_latents(1)
-    each_tile(lambda t: decode_tile(1, t))
+    each_tile(second_decode)
     encode(2)
+    place_rest(1)
     each_tile(far_outer_arrives)
     activate(2)
     encode(3)

time: 163 us -> 166 us (1.018)
  Pallas kernels: 159 us -> 163 us
    pallas_call x1, Pallas kernels: 159 us -> 163 us  [line_body(): pl.pallas_call(functools.partial(line_kernel, tokens, capacity), out_shap...]
where the time goes in v7:
time: 166 us
  Pallas kernels  163 us (98%)
  between operations  2.4 us (1%)
    pallas_call x1, Pallas kernels, line_body(): pl.pallas_call(functools.partial(line_kernel, tokens, capacity), out_shap...  163 us

profile of v7, /device:TPU:0, one launch (start us, length us, event | category | flops | bytes accessed | tf_op | source)
XLA Modules:
  0.0 166.2 jit_solution(5286831840639165903)
XLA Ops:
  0.6 162.6 %shard_map.77 = (f32[256]{0:T(256)}, f32[1,1]{1,0:T(1,128)}) custom-call(bf16[256,1792]{1,0:T(8,128)(2,1)} %act.1, s32[2,256]{1,0:T(2,128)} %bitcast.2, bf16[1792,2048]{1,0:T(8,128)(2,1)} %enc_hbm.1, f32[2048]{0:T(1024)} %enc_bias.1, bf16[2048,1792]{1,0:T(8,128)(2,1)} %dec_hbm.1, f32[1792]{0:T(1024)} %dec_bias.1), custom_call_target="tpu_custom_call" | custom-call | flops 15032385536 | bytes 14680064 | tf_op jit(solution)/shard_map/pallas_call | solution.py:505
  163.2 1.2 copy.10
